TPU v7x, 256 devices: a whole 4x4x8 slice. The times are simulated.
256 devices in a mesh: mesh: 128 (over x_lo, z, y, core), band: 2 (over x_hi).
Axes of the slice: x: 4 (x_hi: 2, x_lo: 2; x = x_hi * 2 + x_lo), y: 4, z: 8, core: 2. Of those that a mesh axis runs over, the one named last changes fastest.
Arguments:
- states: float32 [110592, 512], P('mesh', 'band'), may hold values from -6 to 6
- inv_sqrt_mass: float32 [110592], P('mesh'), may hold values from 0.7 to 1.3
- stiffness: float32 [343, 343], replicated, as said below
- cell_scale: float32 [512], P('mesh'), may hold values from 0.5 to 2
- potential: float32 [512, 343], P('mesh'), may hold values from -1 to 1
- connectivity: int32 [512, 343], P('mesh'), may hold values from 0 to 1295
- shared_rows: int32 [128, 2, 216], P('mesh'), may hold values from 0 to 863
- coefficients: float32 [512, 512], P('band'), may hold values from -0.25 to 0.25
Outputs:
- rotated: float32 [110592, 512], P('mesh', 'band')
Inputs may be any that keep to these rules, and one draw needn't show every extreme that they name: stiffness is symmetric.
All inputs are finite; a program needn't handle non-finite values.
Results may differ from a plain program's by a relative error of at most 0.0001.
Values sent between devices are 32-bit elements; how exact they have to be, the bound alone decides.
A program may use at most 64 MiB of HBM per device.

v0:
```python
import jax
import jax.numpy as jnp
from jax import lax
from jax.sharding import PartitionSpec as P

DEGREE = 3


low_end = -3.0
low_bound = 2.0
high_bound = 14.0


def with_halo(shard, sides, width):
    for axis, dim in sides:
        devices, length = (lax.axis_size(axis), shard.shape[dim])
        up = [(i, (i + 1) % devices) for i in range(devices - 1)]
        down = [(j, i) for i, j in up]
        last = lax.slice_in_dim(shard, length - width, length, axis=dim)
        initial = lax.slice_in_dim(shard, 0, width, axis=dim)
        before = lax.ppermute(last, axis, up)
        after = lax.ppermute(initial, axis, down)
        shard = jnp.concatenate([before, shard, after], axis=dim)
    return shard


def body(
    states, inv_sqrt_mass, stiffness, cell_scale, potential, connectivity, shared_rows, coefficients
):
    own_rows = states.shape[0]
    state_width = states.shape[1]
    shared = shared_rows[0]
    ghost_rows = shared.shape[1]
    flat_slots = connectivity.reshape(-1)

    def apply_operator(values_in):
        scaled = inv_sqrt_mass[:, None] * values_in
        packed = jnp.stack([scaled[shared[0]], scaled[shared[1]]])
        padded = with_halo(packed, (("mesh", 0),), 1)
        extended = jnp.concatenate([scaled, padded[0], padded[3]], axis=0)
        gathered = extended[connectivity]
        cell_terms = (
            cell_scale[:, None, None]
            * jnp.einsum("ij,cjs->cis", stiffness, gathered, precision=lax.Precision.HIGHEST)
            + potential[:, :, None] * gathered
        )
        summed = (
            jnp.zeros((own_rows + 2 * ghost_rows, state_width), jnp.float32)
            .at[flat_slots]
            .add(cell_terms.reshape(-1, state_width))
        )
        returned = jnp.stack(
            [summed[own_rows : own_rows + ghost_rows], summed[own_rows + ghost_rows :]]
        )
        arrived = with_halo(returned, (("mesh", 0),), 1)
        assembled = summed[:own_rows].at[shared[0]].add(arrived[0]).at[shared[1]].add(arrived[3])
        return inv_sqrt_mass[:, None] * assembled

    half_span = (high_bound - low_bound) / 2.0
    centre = (high_bound + low_bound) / 2.0
    sigma_first = half_span / (low_end - centre)
    gamma_term = 2.0 / sigma_first
    current = (apply_operator(states) - centre * states) * (sigma_first / half_span)
    previous = states
    sigma_now = sigma_first
    for step_index in range(DEGREE - 1):
        sigma_next = 1.0 / (gamma_term - sigma_now)
        following = (apply_operator(current) - centre * current) * (
            2.0 * sigma_next / half_span
        ) - sigma_now * sigma_next * previous
        previous = current
        current = following
        sigma_now = sigma_next
    partial_term = jnp.dot(
        current, coefficients, precision=lax.Precision.HIGHEST, preferred_element_type=jnp.float32
    )
    rotated = lax.psum_scatter(partial_term, "band", scatter_dimension=1, tiled=True)
    return rotated


def solution(mesh):
    return jax.shard_map(
        body,
        mesh=mesh,
        in_specs=(
            P("mesh", "band"),
            P("mesh"),
            P(),
            P("mesh"),
            P("mesh", None),
            P("mesh", None),
            P("mesh", None, None),
            P("band", None),
        ),
        out_specs=P("mesh", "band"),
        check_vma=False,
    )
```

profile of v0, /device:TPU:2, one launch (start us, length us, event | category | flops | bytes accessed | tf_op | source)
XLA Modules:
  0.0 212.9 jit_solution(8417597297952670840)
XLA Ops:
  9.6 1.9 collective-permute-start
  12.4 9.6 %collective-permute-start.1 = (f32[1,216,256]{2,1,0:T(8,128)S(1)}, f32[1,216,256]{2,1,0:T(8,128)}, u32[]{:S(2)}, u32[]{:S(2)}) collective-permute-start(f32[1,216,256]{2,1,0:T(8,128)S(1)} %bitcast.72), channel_id=1, source_target_pairs={{2,0},{4,2},{6,4},{8,6},{10,8},{12,10},{14,12},{16,14},{18,16},{20... | collective-permute-start | bytes 663560 | tf_op jit(solution)/shard_map/ppermute | solution.py:22
  22.8 2.7 %collective-permute-done.1 = f32[1,216,256]{2,1,0:T(8,128)} collective-permute-done((f32[1,216,256]{2,1,0:T(8,128)S(1)}, f32[1,216,256]{2,1,0:T(8,128)}, u32[]{:S(2)}, u32[]{:S(2)}) %collective-permute-start.1) | collective-permute-done | bytes 221216 | tf_op jit(solution)/shard_map/ppermute | solution.py:22
  26.5 3.8 %gather_fusion.2 = f32[1372,256]{1,0:T(8,128)S(1)} fusion(f32[1296,256]{1,0:T(8,128)S(1)} %pad_maximum_fusion, s32[2048]{0:T(1024)S(1)} %pad_clamp_fusion), kind=kCustom, calls=%fused_computation.2 | custom fusion | bytes 2815344 | tf_op jit(solution)/shard_map/gather | solution.py:41
  31.0 2.5 %fusion.5 = f32[4,343,256]{2,1,0:T(8,128)S(1)} fusion(f32[4,343,256]{2,1,0:T(8,128)S(1)} %reshape.124, f32[4,343]{1,0:T(4,128)S(1)} %copy-done.6, f32[4]{0:T(128)S(1)} %copy-done.8, f32[343,343]{1,0:T(8,128)S(1)} %copy-done), kind=kOutput, calls=%fused_computation.26 | convolution fusion | flops 1446724608 | bytes 3285956 | tf_op jit(solution)/shard_map/ij,cjs->cis/dot_general | solution.py:44
  33.7 8.4 %scatter_custom_fusion = f32[1296,256]{1,0:T(8,128)S(1)} fusion(s32[1372]{0:T(1024)S(1)} %fusion.38, f32[1372,256]{1,0:T(8,128)S(1)} %reshape.183, f32[]{:T(128)} %constant.11.clone.1), kind=kCustom, calls=%fused_computation.43 | custom fusion | flops 351232 | bytes 1327108 | tf_op jit(solution)/shard_map/scatter-add | solution.py:50
  42.2 8.1 %collective-permute-start.3 = (f32[1,216,256]{2,1,0:T(8,128)S(1)}, f32[1,216,256]{2,1,0:T(8,128)S(1)}, u32[]{:S(2)}, u32[]{:S(2)}) collective-permute-start(f32[1,216,256]{2,1,0:T(8,128)S(1)} %get-tuple-element.9), channel_id=1, source_target_pairs={{2,0},{4,2},{6,4},{8,6},{10,8},{12,10},{14,12},{16,14},{18,16},{20... | collective-permute-start | bytes 663560 | tf_op jit(solution)/shard_map/ppermute | solution.py:22
  50.3 1.9 collective-permute-start.2
  53.2 8.5 %collective-permute-done.2 = f32[1,216,256]{2,1,0:T(8,128)S(1)} collective-permute-done((f32[1,216,256]{2,1,0:T(8,128)S(1)}, f32[1,216,256]{2,1,0:T(8,128)S(1)}, u32[]{:S(2)}, u32[]{:S(2)}) %collective-permute-start.2) | collective-permute-done | bytes 221216 | tf_op jit(solution)/shard_map/ppermute | solution.py:21
  61.8 3.7 %scatter_custom_fusion.1 = f32[864,256]{1,0:T(8,128)} fusion(f32[864,256]{1,0:T(8,128)} %slice.74, s32[216]{0:T(256)S(1)} %bitcast.87, f32[1,216,256]{2,1,0:T(8,128)S(1)} %collective-permute-done.2), kind=kCustom, calls=%fused_computation.71 | custom fusion | flops 55296 | bytes 1105920 | tf_op jit(solution)/shard_map/scatter-add | solution.py:56
  65.5 3.7 %scatter_custom_fusion.2 = f32[864,256]{1,0:T(8,128)} fusion(f32[864,256]{1,0:T(8,128)} %scatter_custom_fusion.1, s32[216]{0:T(256)S(1)} %bitcast.83, f32[1,216,256]{2,1,0:T(8,128)S(1)} %collective-permute-done.3), kind=kCustom, calls=%fused_computation.69 | custom fusion | flops 55296 | bytes 1105920 | tf_op jit(solution)/shard_map/scatter-add | solution.py:56
  72.4 1.9 collective-permute-start.4
  74.4 8.0 %collective-permute-start.5 = (f32[1,216,256]{2,1,0:T(8,128)S(1)}, f32[1,216,256]{2,1,0:T(8,128)S(1)}, u32[]{:S(2)}, u32[]{:S(2)}) collective-permute-start(f32[1,216,256]{2,1,0:T(8,128)S(1)} %bitcast.74), channel_id=1, source_target_pairs={{2,0},{4,2},{6,4},{8,6},{10,8},{12,10},{14,12},{16,14},{18,16},{20... | collective-permute-start | bytes 663560 | tf_op jit(solution)/shard_map/ppermute | solution.py:22
  85.7 3.8 %gather_fusion.5 = f32[1372,256]{1,0:T(8,128)S(1)} fusion(f32[1296,256]{1,0:T(8,128)S(1)} %pad_maximum_fusion.1, s32[2048]{0:T(1024)S(1)} %pad_clamp_fusion), kind=kCustom, calls=%fused_computation.5 | custom fusion | bytes 2815344 | tf_op jit(solution)/shard_map/gather | solution.py:41
  89.7 2.5 %fusion.3 = f32[4,343,256]{2,1,0:T(8,128)S(1)} fusion(f32[4,343,256]{2,1,0:T(8,128)S(1)} %reshape.148, f32[4,343]{1,0:T(4,128)S(1)} %copy-done.6, f32[4]{0:T(128)S(1)} %copy-done.8, f32[343,343]{1,0:T(8,128)S(1)} %copy-done), kind=kOutput, calls=%fused_computation.23 | convolution fusion | flops 1446724608 | bytes 3285956 | tf_op jit(solution)/shard_map/ij,cjs->cis/dot_general | solution.py:44
  92.4 8.4 %scatter_custom_fusion.3 = f32[1296,256]{1,0:T(8,128)S(1)} fusion(s32[1372]{0:T(1024)S(1)} %fusion.38, f32[1372,256]{1,0:T(8,128)S(1)} %reshape.207, f32[]{:T(128)} %constant.11.clone.1), kind=kCustom, calls=%fused_computation.41 | custom fusion | flops 351232 | bytes 1327108 | tf_op jit(solution)/shard_map/scatter-add | solution.py:50
  100.8 1.9 collective-permute-start.6
  102.8 8.0 %collective-permute-start.7 = (f32[1,216,256]{2,1,0:T(8,128)S(1)}, f32[1,216,256]{2,1,0:T(8,128)S(1)}, u32[]{:S(2)}, u32[]{:S(2)}) collective-permute-start(f32[1,216,256]{2,1,0:T(8,128)S(1)} %get-tuple-element.7), channel_id=1, source_target_pairs={{2,0},{4,2},{6,4},{8,6},{10,8},{12,10},{14,12},{16,14},{18,16},{20... | collective-permute-start | bytes 663560 | tf_op jit(solution)/shard_map/ppermute | solution.py:22
  112.5 3.7 %scatter_custom_fusion.4 = f32[864,256]{1,0:T(8,128)} fusion(f32[864,256]{1,0:T(8,128)} %slice.77, s32[216]{0:T(256)S(1)} %bitcast.88, f32[1,216,256]{2,1,0:T(8,128)S(1)} %collective-permute-done.6), kind=kCustom, calls=%fused_computation.67 | custom fusion | flops 55296 | bytes 1105920 | tf_op jit(solution)/shard_map/scatter-add | solution.py:56
  116.2 3.7 %scatter_custom_fusion.5 = f32[864,256]{1,0:T(8,128)} fusion(f32[864,256]{1,0:T(8,128)} %scatter_custom_fusion.4, s32[216]{0:T(256)S(1)} %bitcast.84, f32[1,216,256]{2,1,0:T(8,128)S(1)} %collective-permute-done.7), kind=kCustom, calls=%fused_computation.65 | custom fusion | flops 55296 | bytes 1105920 | tf_op jit(solution)/shard_map/scatter-add | solution.py:56
  119.8 1.8 broadcast_multiply_fusion.1
  123.5 1.9 collective-permute-start.8
  125.4 8.1 %collective-permute-start.9 = (f32[1,216,256]{2,1,0:T(8,128)S(1)}, f32[1,216,256]{2,1,0:T(8,128)S(1)}, u32[]{:S(2)}, u32[]{:S(2)}) collective-permute-start(f32[1,216,256]{2,1,0:T(8,128)S(1)} %bitcast.73), channel_id=1, source_target_pairs={{2,0},{4,2},{6,4},{8,6},{10,8},{12,10},{14,12},{16,14},{18,16},{20... | collective-permute-start | bytes 663560 | tf_op jit(solution)/shard_map/ppermute | solution.py:22
  136.8 3.8 %gather_fusion.8 = f32[1372,256]{1,0:T(8,128)S(1)} fusion(f32[1296,256]{1,0:T(8,128)S(1)} %pad_maximum_fusion.2, s32[2048]{0:T(1024)S(1)} %pad_clamp_fusion), kind=kCustom, calls=%fused_computation.8 | custom fusion | bytes 2815344 | tf_op jit(solution)/shard_map/gather | solution.py:41
  140.7 2.5 %fusion.1 = f32[4,343,256]{2,1,0:T(8,128)S(1)} fusion(f32[4,343,256]{2,1,0:T(8,128)S(1)} %reshape.172, f32[4,343]{1,0:T(4,128)S(1)} %copy-done.6, f32[4]{0:T(128)S(1)} %copy-done.8, f32[343,343]{1,0:T(8,128)S(1)} %copy-done), kind=kOutput, calls=%fused_computation.20 | convolution fusion | flops 1446724608 | bytes 3285956 | tf_op jit(solution)/shard_map/ij,cjs->cis/dot_general | solution.py:44
  143.4 8.4 %scatter_custom_fusion.6 = f32[1296,256]{1,0:T(8,128)S(1)} fusion(s32[1372]{0:T(1024)S(1)} %fusion.38, f32[1372,256]{1,0:T(8,128)S(1)} %reshape.231, f32[]{:T(128)} %constant.11.clone.1), kind=kCustom, calls=%fused_computation.39 | custom fusion | flops 351232 | bytes 1327108 | tf_op jit(solution)/shard_map/scatter-add | solution.py:50
  151.9 1.9 collective-permute-start.10
  153.8 8.0 %collective-permute-start.11 = (f32[1,216,256]{2,1,0:T(8,128)S(1)}, f32[1,216,256]{2,1,0:T(8,128)}, u32[]{:S(2)}, u32[]{:S(2)}) collective-permute-start(f32[1,216,256]{2,1,0:T(8,128)S(1)} %get-tuple-element.5), channel_id=1, source_target_pairs={{2,0},{4,2},{6,4},{8,6},{10,8},{12,10},{14,12},{16,14},{18,16},{20... | collective-permute-start | bytes 663560 | tf_op jit(solution)/shard_map/ppermute | solution.py:22
  163.6 2.5 %scatter_custom_fusion.7 = f32[864,256]{1,0:T(8,128)S(1)} fusion(f32[864,256]{1,0:T(8,128)S(1)} %slice.80, s32[216]{0:T(256)S(1)} %bitcast.89, f32[1,216,256]{2,1,0:T(8,128)} %collective-permute-done.10), kind=kCustom, calls=%fused_computation.63 | custom fusion | flops 55296 | bytes 1105920 | tf_op jit(solution)/shard_map/scatter-add | solution.py:56
  166.1 2.5 %scatter_custom_fusion.8 = f32[864,256]{1,0:T(8,128)S(1)} fusion(f32[864,256]{1,0:T(8,128)S(1)} %scatter_custom_fusion.7, s32[216]{0:T(256)S(1)} %bitcast.85, f32[1,216,256]{2,1,0:T(8,128)} %collective-permute-done.11), kind=kCustom, calls=%fused_computation.61 | custom fusion | flops 55296 | bytes 1105920 | tf_op jit(solution)/shard_map/scatter-add | solution.py:56
  168.7 4.7 %fusion.6 = f32[864,512]{1,0:T(8,128)} fusion(f32[256,512]{1,0:T(8,128)S(1)} %copy-done.4, f32[864,256]{1,0:T(8,128)S(1)} %scatter_custom_fusion.8, f32[864]{0:T(1024)S(1)} %copy-done.5, f32[864,256]{1,0:T(8,128)S(1)} %copy-done.3, f32[864,256]{1,0:T(8,128)} %scatter_custom_fusion.5, f32[864,256]{1,0:T(8,128)} %scatter_custom_fusion.2), kind=kOutput, calls=%fused_computation.30 | convolution fusion | flops 1362272256 | bytes 5836160 | tf_op jit(solution)/shard_map/dot_general | solution.py:74
  173.4 32.6 %reduce-scatter.2.cloned.1.call-done = f32[864,256]{1,0:T(8,128)} async-done(((f32[864,512]{1,0:T(8,128)}), f32[864,256]{1,0:T(8,128)}) %reduce-scatter.2.cloned.1.call-update) | async-done | bytes 884752 | tf_op jit(solution)/shard_map/reduce_scatter | solution.py:77
  (62 shorter events, 23.4 us)
Async XLA Ops:
  6.5 24.0 %copy-start = (f32[343,343]{1,0:T(8,128)S(1)}, f32[343,343]{1,0:T(8,128)}, u32[]{:S(2)}) copy-start(f32[343,343]{1,0:T(8,128)} %param.10) | copy-start | bytes 1411792
  6.5 199.5 %reduce-scatter.2.cloned.1.call-start = ((), (), s32[]{:S(2)}) async-start(), calls=%async_computation.1 | async-start | bytes 2654208 | tf_op jit(solution)/shard_map/reduce_scatter | solution.py:77
  9.6 12.5 %copy-start.7 = (s32[4,343]{1,0:T(4,128)S(1)}, s32[4,343]{1,0:T(4,128)}, u32[]{:S(2)}) copy-start(s32[4,343]{1,0:T(4,128)} %param.13) | copy-start | bytes 16468
  9.6 13.2 %collective-permute-start = (f32[1,216,256]{2,1,0:T(8,128)S(1)}, f32[1,216,256]{2,1,0:T(8,128)S(1)}, u32[]{:S(2)}, u32[]{:S(2)}) collective-permute-start(f32[1,216,256]{2,1,0:T(8,128)S(1)} %bitcast.71), channel_id=1, source_target_pairs={{0,2},{2,4},{4,6},{6,8},{8,10},{10,12},{12,14},{14,16},{16,18},{18... | collective-permute-start | bytes 663560 | tf_op jit(solution)/shard_map/ppermute | solution.py:21
  12.4 13.1 %collective-permute-start.1 = (f32[1,216,256]{2,1,0:T(8,128)S(1)}, f32[1,216,256]{2,1,0:T(8,128)}, u32[]{:S(2)}, u32[]{:S(2)}) collective-permute-start(f32[1,216,256]{2,1,0:T(8,128)S(1)} %bitcast.72), channel_id=1, source_target_pairs={{2,0},{4,2},{6,4},{8,6},{10,8},{12,10},{14,12},{16,14},{18,16},{20... | collective-permute-start | bytes 663560 | tf_op jit(solution)/shard_map/ppermute | solution.py:22
  30.3 0.7 copy-start.6
  30.3 0.7 copy-start.8
  33.7 18.5 %copy-start.5 = (f32[864]{0:T(1024)S(1)}, f32[864]{0:T(1024)}, u32[]{:S(2)}) copy-start(f32[864]{0:T(1024)} %param.9) | copy-start | bytes 10372
  42.2 23.3 %collective-permute-start.3 = (f32[1,216,256]{2,1,0:T(8,128)S(1)}, f32[1,216,256]{2,1,0:T(8,128)S(1)}, u32[]{:S(2)}, u32[]{:S(2)}) collective-permute-start(f32[1,216,256]{2,1,0:T(8,128)S(1)} %get-tuple-element.9), channel_id=1, source_target_pairs={{2,0},{4,2},{6,4},{8,6},{10,8},{12,10},{14,12},{16,14},{18,16},{20... | collective-permute-start | bytes 663560 | tf_op jit(solution)/shard_map/ppermute | solution.py:22
  50.3 11.5 %collective-permute-start.2 = (f32[1,216,256]{2,1,0:T(8,128)S(1)}, f32[1,216,256]{2,1,0:T(8,128)S(1)}, u32[]{:S(2)}, u32[]{:S(2)}) collective-permute-start(f32[1,216,256]{2,1,0:T(8,128)S(1)} %get-tuple-element.10), channel_id=1, source_target_pairs={{0,2},{2,4},{4,6},{6,8},{8,10},{10,12},{12,14},{14,16},{16,18},{18... | collective-permute-start | bytes 663560 | tf_op jit(solution)/shard_map/ppermute | solution.py:21
  53.2 15.9 %copy-start.1 = (f32[864,256]{1,0:T(8,128)S(1)}, f32[864,256]{1,0:T(8,128)}, u32[]{:S(2)}) copy-start(f32[864,256]{1,0:T(8,128)} %param.8) | copy-start | bytes 2654212
  72.4 11.5 %collective-permute-start.4 = (f32[1,216,256]{2,1,0:T(8,128)S(1)}, f32[1,216,256]{2,1,0:T(8,128)S(1)}, u32[]{:S(2)}, u32[]{:S(2)}) collective-permute-start(f32[1,216,256]{2,1,0:T(8,128)S(1)} %bitcast.76), channel_id=1, source_target_pairs={{0,2},{2,4},{4,6},{6,8},{8,10},{10,12},{12,14},{14,16},{16,18},{18... | collective-permute-start | bytes 663560 | tf_op jit(solution)/shard_map/ppermute | solution.py:21
  74.4 11.3 %collective-permute-start.5 = (f32[1,216,256]{2,1,0:T(8,128)S(1)}, f32[1,216,256]{2,1,0:T(8,128)S(1)}, u32[]{:S(2)}, u32[]{:S(2)}) collective-permute-start(f32[1,216,256]{2,1,0:T(8,128)S(1)} %bitcast.74), channel_id=1, source_target_pairs={{2,0},{4,2},{6,4},{8,6},{10,8},{12,10},{14,12},{16,14},{18,16},{20... | collective-permute-start | bytes 663560 | tf_op jit(solution)/shard_map/ppermute | solution.py:22
  100.8 11.6 %collective-permute-start.6 = (f32[1,216,256]{2,1,0:T(8,128)S(1)}, f32[1,216,256]{2,1,0:T(8,128)S(1)}, u32[]{:S(2)}, u32[]{:S(2)}) collective-permute-start(f32[1,216,256]{2,1,0:T(8,128)S(1)} %get-tuple-element.8), channel_id=1, source_target_pairs={{0,2},{2,4},{4,6},{6,8},{8,10},{10,12},{12,14},{14,16},{16,18},{18... | collective-permute-start | bytes 663560 | tf_op jit(solution)/shard_map/ppermute | solution.py:21
  102.8 13.4 %collective-permute-start.7 = (f32[1,216,256]{2,1,0:T(8,128)S(1)}, f32[1,216,256]{2,1,0:T(8,128)S(1)}, u32[]{:S(2)}, u32[]{:S(2)}) collective-permute-start(f32[1,216,256]{2,1,0:T(8,128)S(1)} %get-tuple-element.7), channel_id=1, source_target_pairs={{2,0},{4,2},{6,4},{8,6},{10,8},{12,10},{14,12},{16,14},{18,16},{20... | collective-permute-start | bytes 663560 | tf_op jit(solution)/shard_map/ppermute | solution.py:22
  111.8 8.1 %copy-start.2 = (f32[864,256]{1,0:T(8,128)S(1)}, f32[864,256]{1,0:T(8,128)}, u32[]{:S(2)}) copy-start(f32[864,256]{1,0:T(8,128)} %param.8) | copy-start | bytes 2654212
  123.5 11.5 %collective-permute-start.8 = (f32[1,216,256]{2,1,0:T(8,128)S(1)}, f32[1,216,256]{2,1,0:T(8,128)S(1)}, u32[]{:S(2)}, u32[]{:S(2)}) collective-permute-start(f32[1,216,256]{2,1,0:T(8,128)S(1)} %bitcast.75), channel_id=1, source_target_pairs={{0,2},{2,4},{4,6},{6,8},{8,10},{10,12},{12,14},{14,16},{16,18},{18... | collective-permute-start | bytes 663560 | tf_op jit(solution)/shard_map/ppermute | solution.py:21
  125.4 11.3 %collective-permute-start.9 = (f32[1,216,256]{2,1,0:T(8,128)S(1)}, f32[1,216,256]{2,1,0:T(8,128)S(1)}, u32[]{:S(2)}, u32[]{:S(2)}) collective-permute-start(f32[1,216,256]{2,1,0:T(8,128)S(1)} %bitcast.73), channel_id=1, source_target_pairs={{2,0},{4,2},{6,4},{8,6},{10,8},{12,10},{14,12},{16,14},{18,16},{20... | collective-permute-start | bytes 663560 | tf_op jit(solution)/shard_map/ppermute | solution.py:22
  151.9 11.7 %collective-permute-start.10 = (f32[1,216,256]{2,1,0:T(8,128)S(1)}, f32[1,216,256]{2,1,0:T(8,128)}, u32[]{:S(2)}, u32[]{:S(2)}) collective-permute-start(f32[1,216,256]{2,1,0:T(8,128)S(1)} %get-tuple-element.6), channel_id=1, source_target_pairs={{0,2},{2,4},{4,6},{6,8},{8,10},{10,12},{12,14},{14,16},{16,18},{18... | collective-permute-start | bytes 663560 | tf_op jit(solution)/shard_map/ppermute | solution.py:21
  153.8 12.3 %collective-permute-start.11 = (f32[1,216,256]{2,1,0:T(8,128)S(1)}, f32[1,216,256]{2,1,0:T(8,128)}, u32[]{:S(2)}, u32[]{:S(2)}) collective-permute-start(f32[1,216,256]{2,1,0:T(8,128)S(1)} %get-tuple-element.5), channel_id=1, source_target_pairs={{2,0},{4,2},{6,4},{8,6},{10,8},{12,10},{14,12},{16,14},{18,16},{20... | collective-permute-start | bytes 663560 | tf_op jit(solution)/shard_map/ppermute | solution.py:22
  161.9 6.7 %copy-start.3 = (f32[864,256]{1,0:T(8,128)S(1)}, f32[864,256]{1,0:T(8,128)}, u32[]{:S(2)}) copy-start(f32[864,256]{1,0:T(8,128)} %param.8) | copy-start | bytes 2654212
  161.9 6.7 %copy-start.4 = (f32[256,512]{1,0:T(8,128)S(1)}, f32[256,512]{1,0:T(8,128)}, u32[]{:S(2)}) copy-start(f32[256,512]{1,0:T(8,128)} %param.15) | copy-start | bytes 1572868
Sparse Core Ops, SparseCore 0:
  173.5 32.4 reduce-scatter.1
where the time goes:
time: 215 us; the launch traced here: 213 us
  starting transfers between devices  61.5 us (29%)
  waiting for transfers between devices  53.2 us (25%)
  other arithmetic  51.5 us (24%)
  local copies, waits for them, and re-layouts  20.5 us (10%)
  between operations  13.8 us (6%)
  matrix products  12.3 us (6%)
    ppermute x6, starting transfers between devices, with_halo(): after = lax.ppermute(initial, axis, down)  50 us
    reduce_scatter x1, waiting for transfers between devices, body(): lax.psum_scatter(partial_term, 'band', scatter_dimension=1, tiled=True)  32.6 us
    scatter-add x3, other arithmetic, apply_operator(): summed = jnp.zeros((own_rows + 2 * ghost_rows, state_width), jnp.float32)...  25.2 us
    scatter-add x6, other arithmetic, apply_operator(): summed[:own_rows].at[shared[0]].add(arrived[0]).at[shared[1]]  19.7 us
    ppermute x6, waiting for transfers between devices, with_halo(): before = lax.ppermute(last, axis, up)  14.4 us
    gather x6, local copies, waits for them, and re-layouts, apply_operator(): gathered = extended[connectivity]  11.8 us
    ppermute x6, starting transfers between devices, with_halo(): before = lax.ppermute(last, axis, up)  11.5 us
    dot_general x3, matrix products, apply_operator(): jnp.einsum('ij,cjs->cis', stiffness, gathered, precision=lax.Precision.HI...  7.62 us
  transfers between devices with their start and end apart: 13, of which 10 were waited for; matrix products, arithmetic and copies ran while one was open for 6% of the time, Pallas kernels for 0%

commit v1 on v0

v1 whole, which is shorter than its diff:
```python
import jax
import jax.numpy as jnp
from jax import lax
from jax.experimental import pallas as pl
from jax.experimental.pallas import tpu as pltpu
from jax.sharding import PartitionSpec as P

MESH = pl.DeviceIdType.MESH
F32, BF16 = jnp.float32, jnp.bfloat16

DEGREE = 3
OWN = 864
GHOST = 216
NODES = OWN + 2 * GHOST
NPE = 343
PAD = 384
CELLS = 4
W = 128
BANDW = 256

low_end = -3.0
low_bound = 2.0
high_bound = 14.0

half_span = (high_bound - low_bound) / 2.0
centre = (high_bound + low_bound) / 2.0
sigma_first = half_span / (low_end - centre)
gamma_term = 2.0 / sigma_first


def chebyshev():
    rows = [(sigma_first / half_span, 0.0)]
    now = sigma_first
    for _ in range(DEGREE - 1):
        later = 1.0 / (gamma_term - now)
        rows.append((2.0 * later / half_span, now * later))
        now = later
    return rows


COEFS = chebyshev()


def dot(a, b):
    return jnp.dot(a, b, preferred_element_type=F32)


def dot_nt(a, b):
    return lax.dot_general(a, b, (((1,), (1,)), ((), ())), preferred_element_type=F32)


def split(x):
    high = x.astype(BF16)
    return high, (x - high.astype(F32)).astype(BF16)


def pair(x):
    return jnp.concatenate(split(x), axis=1)


def fold(y):
    return y[:, :W] + y[:, W:]


def apply_pair(high, low, packed):
    return fold(dot(high, packed)) + dot(low, packed[:, :W])


def kernel(
    parts,
    states,
    mass,
    stiffness,
    scale,
    potential,
    slots,
    shared,
    coefficients,
    out,
    stiff_pad,
    slot_pad,
    pot_pad,
    turn,
    mass_cols,
    one_hot,
    prod_own_hi,
    prod_own_lo,
    prod_ghost_hi,
    prod_ghost_lo,
    own_hi,
    own_lo,
    ghost_hi,
    ghost_lo,
    pick,
    place,
    band_out,
    band_in,
    value,
    before,
    pre,
    acc,
    ghost_out,
    ghost_in,
    back_out,
    back_in,
    band_send,
    band_recv,
    ghost_send,
    ghost_recv,
    back_send,
    back_recv,
):
    me = lax.axis_index("mesh")
    band = lax.axis_index("band")
    lower = (lax.rem(me + parts - 1, parts), band)
    upper = (lax.rem(me + 1, parts), band)
    other = (me, 1 - band)

    barrier = pltpu.get_barrier_semaphore()
    for device in (other, lower, upper):
        pl.semaphore_signal(barrier, inc=1, device_id=device, device_id_type=MESH)

    def band_copy(j):
        return pltpu.make_async_remote_copy(
            src_ref=band_out.at[j],
            dst_ref=band_in.at[j],
            send_sem=band_send.at[j],
            recv_sem=band_recv.at[j],
            device_id=other,
            device_id_type=MESH,
        )

    def chain_copies(src, dst, send, recv, k, j):
        down = pltpu.make_async_remote_copy(
            src_ref=src.at[k, j, pl.ds(0, GHOST)],
            dst_ref=dst.at[k, j, pl.ds(GHOST, GHOST)],
            send_sem=send.at[k, j, 0],
            recv_sem=recv.at[k, j, 0],
            device_id=lower,
            device_id_type=MESH,
        )
        up = pltpu.make_async_remote_copy(
            src_ref=src.at[k, j, pl.ds(GHOST, GHOST)],
            dst_ref=dst.at[k, j, pl.ds(0, GHOST)],
            send_sem=send.at[k, j, 1],
            recv_sem=recv.at[k, j, 1],
            device_id=upper,
            device_id_type=MESH,
        )
        return down, up

    def ghost_copies(k, j):
        return chain_copies(ghost_out, ghost_in, ghost_send, ghost_recv, k, j)

    def back_copies(k, j):
        return chain_copies(back_out, back_in, back_send, back_recv, k, j)

    x_hi, x_lo = split(states[...])

    def rotated_chunk(which, j):
        at = pl.multiple_of(which * BANDW + j * W, W)
        c_hi, c_lo = split(coefficients[:, pl.ds(at, W)])
        return fold(dot(x_hi, jnp.concatenate([c_hi, c_lo], axis=1))) + dot(x_lo, c_hi)

    for j in range(2):
        band_out[j] = rotated_chunk(1 - band, j)
        if j == 0:
            pl.semaphore_wait(barrier, 3)
        band_copy(j).start()
    for j in range(2):
        value[j] = rotated_chunk(band, j)

    turn[...] = jnp.zeros_like(turn)
    turn[:, :OWN] = jnp.broadcast_to(mass[...], (W, OWN))
    mass_cols[...] = turn[...].T[:OWN]

    rows = shared[...]
    place[...] = jnp.where(
        lax.broadcasted_iota(jnp.int32, (OWN, 2 * GHOST), 0) == rows, 1.0, 0.0
    ).astype(BF16)
    turn[:, : 2 * GHOST] = jnp.broadcast_to(rows.astype(F32), (W, 2 * GHOST))
    columns = turn[:, :512].T[: 2 * GHOST].astype(jnp.int32)
    for at in range(0, OWN, W):
        width = min(W, OWN - at)
        pick[:, at : at + width] = jnp.where(
            lax.broadcasted_iota(jnp.int32, (2 * GHOST, width), 1) + at == columns[:, :width],
            1.0,
            0.0,
        ).astype(BF16)

    stiff_pad[...] = jnp.zeros_like(stiff_pad)
    stiff_pad[:NPE, :NPE] = stiffness[...]
    slot_pad[...] = jnp.full(slot_pad.shape, -1, jnp.int32)
    drawn = slots[...]
    absent = ((me == 0) & (drawn >= OWN) & (drawn < OWN + GHOST)) | (
        (me == parts - 1) & (drawn >= OWN + GHOST)
    )
    slot_pad[:CELLS, :NPE] = jnp.where(absent, -1, drawn)
    pot_pad[...] = jnp.zeros_like(pot_pad)
    pot_pad[:CELLS, :NPE] = potential[...]

    @pl.loop(0, CELLS)
    def _(c):
        at = pl.multiple_of(c * PAD, PAD)
        row = slot_pad[pl.ds(c, 1), :]
        hot = jnp.where(
            lax.broadcasted_iota(jnp.int32, (NODES, PAD), 0) == row, 1.0, 0.0
        ).astype(BF16)
        one_hot[:, pl.ds(at, PAD)] = hot
        diagonal = lax.broadcasted_iota(jnp.int32, (PAD, PAD), 0) == lax.broadcasted_iota(
            jnp.int32, (PAD, PAD), 1
        )
        cell = scale[c] * stiff_pad[...] + jnp.where(diagonal, pot_pad[pl.ds(c, 1), :], 0.0)
        stacked = jnp.concatenate(split(cell), axis=0)
        for part, high, low in (
            (hot[:OWN], prod_own_hi, prod_own_lo),
            (hot[OWN:], prod_ghost_hi, prod_ghost_lo),
        ):
            both = dot_nt(stacked, part)
            high[pl.ds(at, PAD), :], low[pl.ds(at, PAD), :] = split(both[:PAD] + both[PAD:])

    for high, low, to_hi, to_lo, length in (
        (prod_own_hi, prod_own_lo, own_hi, own_lo, OWN),
        (prod_ghost_hi, prod_ghost_lo, ghost_hi, ghost_lo, 2 * GHOST),
    ):
        for at in range(0, length, 256):
            cols = slice(at, min(at + 256, length))
            block = dot(one_hot[...], high[:, cols]) + dot(one_hot[...], low[:, cols])
            to_hi[:, cols], to_lo[:, cols] = split(block)

    def scatter_own(k, j):
        packed = pair(mass_cols[...] * value[j])
        ghost_out[k, j] = fold(dot(pick[...], packed))
        for copy in ghost_copies(k, j):
            copy.start()
        pre[j] = apply_pair(own_hi[...], own_lo[...], packed)

    def begin(j):
        band_copy(j).wait_recv()
        value[j] = value[j] + band_in[j]
        before[j] = jnp.zeros((OWN, W), F32)
        scatter_own(0, j)

    def ghost_step(k, j):
        for copy in ghost_copies(k, j):
            copy.wait_recv()
        packed = pair(ghost_in[k, j])
        back_out[k, j] = pre[j, OWN:] + apply_pair(ghost_hi[OWN:], ghost_lo[OWN:], packed)
        for copy in back_copies(k, j):
            copy.start()
        acc[j] = pre[j, :OWN] + apply_pair(ghost_hi[:OWN], ghost_lo[:OWN], packed)

    def back_step(k, j, front, past):
        for copy in back_copies(k, j):
            copy.wait_recv()
        u = mass_cols[...] * (acc[j] + fold(dot(place[...], pair(back_in[k, j]))))
        now = value[j]
        return (u - centre * now) * front - past * before[j], now

    def advance(k, j):
        front = jnp.where(k == 0, COEFS[0][0], COEFS[1][0])
        past = jnp.where(k == 0, COEFS[0][1], COEFS[1][1])
        following, now = back_step(k, j, front, past)
        before[j] = now
        value[j] = following
        scatter_own(k + 1, j)

    begin(0)
    ghost_step(0, 0)
    begin(1)

    @pl.loop(0, DEGREE - 1)
    def _(k):
        advance(k, 0)
        ghost_step(k, 1)
        ghost_step(k + 1, 0)
        advance(k, 1)

    last = DEGREE - 1
    out[:, :W] = back_step(last, 0, *COEFS[last])[0]
    ghost_step(last, 1)
    out[:, W:] = back_step(last, 1, *COEFS[last])[0]

    for j in range(2):
        band_copy(j).wait_send()

    @pl.loop(0, DEGREE)
    def _(k):
        for j in range(2):
            for copy in ghost_copies(k, j) + back_copies(k, j):
                copy.wait_send()


def solution(mesh):
    parts = mesh.shape["mesh"]
    vmem = pl.BlockSpec(memory_space=pltpu.VMEM)
    smem = pl.BlockSpec(memory_space=pltpu.SMEM)
    dma = pltpu.SemaphoreType.DMA

    def body(states, mass, stiffness, scale, potential, slots, shared, coefficients):
        def run(*refs):
            kernel(parts, *refs)

        return pl.pallas_call(
            run,
            out_shape=jax.ShapeDtypeStruct((OWN, BANDW), F32),
            in_specs=[vmem, vmem, vmem, smem, vmem, vmem, vmem, vmem],
            out_specs=vmem,
            scratch_shapes=[
                pltpu.VMEM((PAD, PAD), F32),
                pltpu.VMEM((8, PAD), jnp.int32),
                pltpu.VMEM((8, PAD), F32),
                pltpu.VMEM((W, 896), F32),
                pltpu.VMEM((OWN, W), F32),
                pltpu.VMEM((NODES, CELLS * PAD), BF16),
                pltpu.VMEM((CELLS * PAD, OWN), BF16),
                pltpu.VMEM((CELLS * PAD, OWN), BF16),
                pltpu.VMEM((CELLS * PAD, 2 * GHOST), BF16),
                pltpu.VMEM((CELLS * PAD, 2 * GHOST), BF16),
                pltpu.VMEM((NODES, OWN), BF16),
                pltpu.VMEM((NODES, OWN), BF16),
                pltpu.VMEM((NODES, 2 * GHOST), BF16),
                pltpu.VMEM((NODES, 2 * GHOST), BF16),
                pltpu.VMEM((2 * GHOST, OWN), BF16),
                pltpu.VMEM((OWN, 2 * GHOST), BF16),
                pltpu.VMEM((2, OWN, W), F32),
                pltpu.VMEM((2, OWN, W), F32),
                pltpu.VMEM((2, OWN, W), F32),
                pltpu.VMEM((2, OWN, W), F32),
                pltpu.VMEM((2, NODES, W), F32),
                pltpu.VMEM((2, OWN, W), F32),
                pltpu.VMEM((DEGREE, 2, 2 * GHOST, W), F32),
                pltpu.VMEM((DEGREE, 2, 2 * GHOST, W), F32),
                pltpu.VMEM((DEGREE, 2, 2 * GHOST, W), F32),
                pltpu.VMEM((DEGREE, 2, 2 * GHOST, W), F32),
                dma((2,)),
                dma((2,)),
                dma((DEGREE, 2, 2)),
                dma((DEGREE, 2, 2)),
                dma((DEGREE, 2, 2)),
                dma((DEGREE, 2, 2)),
            ],
            compiler_params=pltpu.CompilerParams(
                collective_id=0, has_side_effects=True, vmem_limit_bytes=56 * 2**20
            ),
        )(
            states,
            mass.reshape(1, OWN),
            stiffness,
            scale,
            potential,
            slots,
            shared.reshape(1, 2 * GHOST),
            coefficients,
        )

    return jax.shard_map(
        body,
        mesh=mesh,
        in_specs=(
            P("mesh", "band"),
            P("mesh"),
            P(),
            P("mesh"),
            P("mesh", None),
            P("mesh", None),
            P("mesh", None, None),
            P("band", None),
        ),
        out_specs=P("mesh", "band"),
        check_vma=False,
    )
```

time: 215 us -> 80.5 us (0.37)
  Pallas kernels: 0 us -> 76.2 us
  starting transfers between devices: 61.5 us -> 0 us
  waiting for transfers between devices: 53.2 us -> 0 us
  other arithmetic: 51.5 us -> 0 us
  local copies, waits for them, and re-layouts: 20.5 us -> 4.09 us
  between operations: 13.8 us -> 0.01 us
  matrix products: 12.3 us -> 0 us
    pallas_call x0 -> x1, Pallas kernels: none -> 76.2 us  [body(): pl.pallas_call(run, out_shape=jax.ShapeDtypeStruct((OWN, BANDW), F32), in...]
    ppermute x12 -> x0, starting transfers between devices: 61.5 us -> none  [the longest x6 50 us: with_halo(): after = lax.ppermute(initial, axis, down)]
    scatter-add x9 -> x0, other arithmetic: 44.8 us -> none  [the longest x3 25.2 us: apply_operator(): summed = jnp.zeros((own_rows + 2 * ghost_rows, state_width), jnp.float32)...]
    reduce_scatter x1 -> x0, waiting for transfers between devices: 32.6 us -> none  [body(): lax.psum_scatter(partial_term, 'band', scatter_dimension=1, tiled=True)]
    ppermute x12 -> x0, waiting for transfers between devices: 20.6 us -> none  [the longest x6 14.4 us: with_halo(): before = lax.ppermute(last, axis, up)]
    gather x12 -> x0, local copies, waits for them, and re-layouts: 17.2 us -> none  [the longest x6 11.8 us: apply_operator(): gathered = extended[connectivity]]
    dot_general x4 -> x0, matrix products: 12.3 us -> none  [the longest x3 7.62 us: apply_operator(): jnp.einsum('ij,cjs->cis', stiffness, gathered, precision=lax.Precision.HI...]
    mul x4 -> x0, other arithmetic: 4.61 us -> none  [apply_operator(): scaled = inv_sqrt_mass[:, None] * values_in]
  transfers between devices with their start and end apart: 13 -> 0, of which waited for: 10 -> 0; matrix products, arithmetic and copies ran while one was open for 6% -> 0% of each run, Pallas kernels for 0% -> 0%
where the time goes in v1:
time: 80.5 us; the launch traced here: 80.3 us
  Pallas kernels  76.2 us (95%)
  local copies, waits for them, and re-layouts  4.09 us (5%)
    pallas_call x1, Pallas kernels, body(): pl.pallas_call(run, out_shape=jax.ShapeDtypeStruct((OWN, BANDW), F32), in...  76.2 us
    unnamed x3, local copies, waits for them, and re-layouts  2.14 us

profile of v1, /device:TPU:2, one launch (start us, length us, event | category | flops | bytes accessed | tf_op | source)
XLA Modules:
  0.0 80.3 jit_solution(10735524411326337430)
XLA Ops:
  0.0 0.0 copy-start
  0.0 1.4 %reshape.7.refs_6_ = s32[1,432]{1,0:T(1,128)} reshape(s32[1,2,216]{2,1,0:T(2,128)} %param.14) | data formatting | bytes 3456 | tf_op jit(solution)/shard_map/reshape | solution.py:353
  1.4 0.0 copy-done
  1.4 0.6 reshape.6.refs_1_
  2.0 76.2 %shard_map.82 = f32[864,256]{1,0:T(8,128)} custom-call(f32[864,256]{1,0:T(8,128)} %refs_0_.1, f32[1,864]{1,0:T(1,128)} %reshape.6.refs_1_, f32[343,343]{1,0:T(8,128)} %refs_2_.1, f32[4]{0:T(128)} %refs_3_.1, f32[4,343]{1,0:T(4,128)} %refs_4_.1, s32[4,343]{1,0:T(4,128)} %refs_5_.1, s32[1,432]{1,0:T(1,128)} %reshape.7.refs_6_, f32[256,512]{1,0:T(8,128)} %refs_7_.1), custom_call_target="tpu_custom_call" | custom-call | tf_op jit(solution)/shard_map/pallas_call | solution.py:304
  78.2 2.1 %copy.10 = f32[864,256]{1,0:T(8,128)} copy(f32[864,256]{1,0:T(8,128)} %shard_map.82) | data formatting | bytes 1769472
Async XLA Ops:
  0.0 1.4 %copy-start = (f32[864]{0:T(1024)S(1)}, f32[864]{0:T(1024)}, u32[]{:S(2)}) copy-start(f32[864]{0:T(1024)} %param.9) | copy-start | bytes 10372

commit v2 on v1

--- a/solution.py
+++ b/solution.py
@@ -112,12 +112,13 @@
 ):
     me = lax.axis_index("mesh")
     band = lax.axis_index("band")
-    lower = (lax.rem(me + parts - 1, parts), band)
-    upper = (lax.rem(me + 1, parts), band)
+    core = lax.rem(me, 2)
+    near = (me + 1 - 2 * core, band)
+    far = (lax.rem(me + parts - 1 + 2 * core, parts), band)
     other = (me, 1 - band)
 
     barrier = pltpu.get_barrier_semaphore()
-    for device in (other, lower, upper):
+    for device in (other, far, near):
         pl.semaphore_signal(barrier, inc=1, device_id=device, device_id_type=MESH)
 
     def band_copy(j):
@@ -131,23 +132,21 @@
         )
 
     def chain_copies(src, dst, send, recv, k, j):
-        down = pltpu.make_async_remote_copy(
-            src_ref=src.at[k, j, pl.ds(0, GHOST)],
-            dst_ref=dst.at[k, j, pl.ds(GHOST, GHOST)],
-            send_sem=send.at[k, j, 0],
-            recv_sem=recv.at[k, j, 0],
-            device_id=lower,
-            device_id_type=MESH,
-        )
-        up = pltpu.make_async_remote_copy(
-            src_ref=src.at[k, j, pl.ds(GHOST, GHOST)],
-            dst_ref=dst.at[k, j, pl.ds(0, GHOST)],
-            send_sem=send.at[k, j, 1],
-            recv_sem=recv.at[k, j, 1],
-            device_id=upper,
-            device_id_type=MESH,
-        )
-        return down, up
+        copies = []
+        for edge, device, row in ((0, far, core * GHOST), (1, near, (1 - core) * GHOST)):
+            row = pl.multiple_of(row, 8)
+            there = pl.multiple_of(GHOST - row, 8)
+            copies.append(
+                pltpu.make_async_remote_copy(
+                    src_ref=src.at[k, j, pl.ds(row, GHOST)],
+                    dst_ref=dst.at[k, j, pl.ds(there, GHOST)],
+                    send_sem=send.at[k, j, edge],
+                    recv_sem=recv.at[k, j, edge],
+                    device_id=device,
+                    device_id_type=MESH,
+                )
+            )
+        return copies
 
     def ghost_copies(k, j):
         return chain_copies(ghost_out, ghost_in, ghost_send, ghost_recv, k, j)
@@ -171,10 +170,10 @@
         value[j] = rotated_chunk(band, j)
 
     turn[...] = jnp.zeros_like(turn)
-    turn[:, :OWN] = jnp.broadcast_to(mass[...], (W, OWN))
+    turn[:, :OWN] = jnp.broadcast_to(mass[...].reshape(1, OWN), (W, OWN))
     mass_cols[...] = turn[...].T[:OWN]
 
-    rows = shared[...]
+    rows = jnp.concatenate([shared[0, 0:1, :], shared[0, 1:2, :]], axis=1)
     place[...] = jnp.where(
         lax.broadcasted_iota(jnp.int32, (OWN, 2 * GHOST), 0) == rows, 1.0, 0.0
     ).astype(BF16)
@@ -219,21 +218,33 @@
             both = dot_nt(stacked, part)
             high[pl.ds(at, PAD), :], low[pl.ds(at, PAD), :] = split(both[:PAD] + both[PAD:])
 
-    for high, low, to_hi, to_lo, length in (
-        (prod_own_hi, prod_own_lo, own_hi, own_lo, OWN),
-        (prod_ghost_hi, prod_ghost_lo, ghost_hi, ghost_lo, 2 * GHOST),
-    ):
-        for at in range(0, length, 256):
-            cols = slice(at, min(at + 256, length))
-            block = dot(one_hot[...], high[:, cols]) + dot(one_hot[...], low[:, cols])
-            to_hi[:, cols], to_lo[:, cols] = split(block)
+    def block(rows, cols, high, low):
+        left = one_hot[rows, :]
+        return dot(left, high[:, cols]) + dot(left, low[:, cols])
+
+    def own_block(at):
+        end = min(at + 256, OWN)
+        whole = block(slice(at, NODES), slice(at, end), prod_own_hi, prod_own_lo)
+        own_hi[at:, at:end], own_lo[at:, at:end] = split(whole)
+        if end < OWN:
+            flipped = whole[end - at : OWN - at].T
+            own_hi[at:end, end:], own_lo[at:end, end:] = split(flipped)
+        ghost_hi[at:end], ghost_lo[at:end] = split(whole[OWN - at :].T)
+
+    def ghost_block():
+        for at in (0, 256):
+            cols = slice(at, min(at + 256, 2 * GHOST))
+            square = block(slice(OWN, NODES), cols, prod_ghost_hi, prod_ghost_lo)
+            ghost_hi[OWN:, cols], ghost_lo[OWN:, cols] = split(square)
 
     def scatter_own(k, j):
         packed = pair(mass_cols[...] * value[j])
         ghost_out[k, j] = fold(dot(pick[...], packed))
         for copy in ghost_copies(k, j):
             copy.start()
-        pre[j] = apply_pair(own_hi[...], own_lo[...], packed)
+
+    def own_product(j):
+        pre[j] = apply_pair(own_hi[...], own_lo[...], pair(mass_cols[...] * value[j]))
 
     def begin(j):
         band_copy(j).wait_recv()
@@ -257,6 +268,13 @@
         now = value[j]
         return (u - centre * now) * front - past * before[j], now
 
+    def finish(j):
+        for copy in back_copies(last, j):
+            copy.wait_recv()
+        u = mass_cols[...] * (acc[j] + fold(dot(place[...], pair(back_in[last, j]))))
+        front, past = COEFS[last]
+        out[:, j * W : (j + 1) * W] = (u - centre * value[j]) - (past / front) * before[j]
+
     def advance(k, j):
         front = jnp.where(k == 0, COEFS[0][0], COEFS[1][0])
         past = jnp.where(k == 0, COEFS[0][1], COEFS[1][1])
@@ -264,10 +282,18 @@
         before[j] = now
         value[j] = following
         scatter_own(k + 1, j)
-
+        own_product(j)
+
+    own_block(0)
+    ghost_block()
     begin(0)
+    own_block(256)
+    own_block(512)
+    own_block(768)
+    own_product(0)
     ghost_step(0, 0)
     begin(1)
+    own_product(1)
 
     @pl.loop(0, DEGREE - 1)
     def _(k):
@@ -277,9 +303,9 @@
         advance(k, 1)
 
     last = DEGREE - 1
-    out[:, :W] = back_step(last, 0, *COEFS[last])[0]
+    finish(0)
     ghost_step(last, 1)
-    out[:, W:] = back_step(last, 1, *COEFS[last])[0]
+    finish(1)
 
     for j in range(2):
         band_copy(j).wait_send()
@@ -301,7 +327,7 @@
         def run(*refs):
             kernel(parts, *refs)
 
-        return pl.pallas_call(
+        filtered = pl.pallas_call(
             run,
             out_shape=jax.ShapeDtypeStruct((OWN, BANDW), F32),
             in_specs=[vmem, vmem, vmem, smem, vmem, vmem, vmem, vmem],
@@ -345,14 +371,15 @@
             ),
         )(
             states,
-            mass.reshape(1, OWN),
+            mass,
             stiffness,
             scale,
             potential,
             slots,
-            shared.reshape(1, 2 * GHOST),
+            shared,
             coefficients,
         )
+        return filtered * COEFS[-1][0]
 
     return jax.shard_map(
         body,

time: 80.5 us -> 71.5 us (0.89)
  Pallas kernels: 76.2 us -> 68.5 us
  local copies, waits for them, and re-layouts: 4.09 us -> 0 us
  other arithmetic: 0 us -> 2.16 us
    pallas_call x1, Pallas kernels: 76.2 us -> 68.5 us  [body(): pl.pallas_call(run, out_shape=jax.ShapeDtypeStruct((OWN, BANDW), F32), in...]
    mul x0 -> x1, other arithmetic: none -> 2.16 us  [body(): return filtered * COEFS[-1][0]]
    unnamed x3 -> x0, local copies, waits for them, and re-layouts: 2.14 us -> none
    reshape x2 -> x0, local copies, waits for them, and re-layouts: 1.95 us -> none  [the longest x1 1.37 us: body(): shared.reshape(1, 2 * GHOST)]
where the time goes in v2:
time: 71.5 us; the launch traced here: 70.7 us
  Pallas kernels  68.5 us (96%)
  other arithmetic  2.16 us (3%)
    pallas_call x1, Pallas kernels, body(): pl.pallas_call(run, out_shape=jax.ShapeDtypeStruct((OWN, BANDW), F32), in...  68.5 us
    mul x1, other arithmetic, body(): return filtered * COEFS[-1][0]  2.16 us

profile of v2, /device:TPU:2, one launch (start us, length us, event | category | flops | bytes accessed | tf_op | source)
XLA Modules:
  0.0 70.7 jit_solution(2281457697588718003)
XLA Ops:
  0.0 68.5 %shard_map.82 = f32[864,256]{1,0:T(8,128)} custom-call(f32[864,256]{1,0:T(8,128)} %refs_0_.1, f32[864]{0:T(1024)} %refs_1_.1, f32[343,343]{1,0:T(8,128)} %refs_2_.1, f32[4]{0:T(128)} %refs_3_.1, f32[4,343]{1,0:T(4,128)} %refs_4_.1, s32[4,343]{1,0:T(4,128)} %refs_5_.1, s32[1,2,216]{2,1,0:T(2,128)} %refs_6_.1, f32[256,512]{1,0:T(8,128)} %refs_7_.1), custom_call_target="tpu_custom_call" | custom-call | tf_op jit(solution)/shard_map/pallas_call | solution.py:330
  68.5 2.2 %broadcast_multiply_fusion = f32[864,256]{1,0:T(8,128)} fusion(f32[864,256]{1,0:T(8,128)} %shard_map.82), kind=kLoop, calls=%fused_computation | loop fusion | flops 221184 | bytes 1769472 | tf_op jit(solution)/shard_map/mul | solution.py:382

commit v3 on v2

v3 whole, which is shorter than its diff:
```python
import jax
import jax.numpy as jnp
from jax import lax
from jax.experimental import pallas as pl
from jax.experimental.pallas import tpu as pltpu
from jax.sharding import PartitionSpec as P

MESH = pl.DeviceIdType.MESH
F32, BF16 = jnp.float32, jnp.bfloat16

DEGREE = 3
OWN = 864
GHOST = 216
EDGE = 224
BOTH = 2 * EDGE
ROWS = OWN + BOTH
NPE = 343
PAD = 384
CELLS = 4
W = 128
BANDW = 256
FAR, NEAR = 0, 1

low_end = -3.0
low_bound = 2.0
high_bound = 14.0

half_span = (high_bound - low_bound) / 2.0
centre = (high_bound + low_bound) / 2.0
sigma_first = half_span / (low_end - centre)
gamma_term = 2.0 / sigma_first


def chebyshev():
    rows = [(sigma_first / half_span, 0.0)]
    now = sigma_first
    for _ in range(DEGREE - 1):
        later = 1.0 / (gamma_term - now)
        rows.append((2.0 * later / half_span, now * later))
        now = later
    return rows


COEFS = chebyshev()


def dot(a, b):
    return jnp.dot(a, b, preferred_element_type=F32)


def dot_nt(a, b):
    return lax.dot_general(a, b, (((1,), (1,)), ((), ())), preferred_element_type=F32)


def split(x):
    high = x.astype(BF16)
    return high, (x - high.astype(F32)).astype(BF16)


def pair(x):
    return jnp.concatenate(split(x), axis=1)


def fold(y):
    return y[:, :W] + y[:, W:]


def apply_pair(high, low, packed):
    return fold(dot(high, packed)) + dot(low, packed[:, :W])


def iota(shape, dim):
    return lax.broadcasted_iota(jnp.int32, shape, dim)


def hot(mask):
    return jnp.where(mask, 1.0, 0.0).astype(BF16)


def kernel(
    parts,
    states,
    mass,
    stiffness,
    scale,
    potential,
    slots,
    shared,
    coefficients,
    out,
    stiff_pad,
    slot_pad,
    pot_pad,
    list_pad,
    turn,
    mass_sq,
    mass_inv,
    far_sq,
    one_hot,
    prod_own_hi,
    prod_own_lo,
    prod_edge_hi,
    prod_edge_lo,
    own_hi,
    own_lo,
    edge_hi,
    edge_lo,
    pick,
    place,
    same,
    info_out,
    info_in,
    band_out,
    band_in,
    now,
    before,
    pre,
    acc,
    stack,
    echo,
    ghost_out,
    ghost_in,
    back_out,
    back_in,
    info_sems,
    band_send,
    band_recv,
    ghost_send,
    ghost_recv,
    back_send,
    back_recv,
):
    me = lax.axis_index("mesh")
    band = lax.axis_index("band")
    core = lax.rem(me, 2)
    near = (me + 1 - 2 * core, band)
    far = (lax.rem(me + parts - 1 + 2 * core, parts), band)
    other = (me, 1 - band)

    barrier = pltpu.get_barrier_semaphore()
    for device in (other, far, near):
        pl.semaphore_signal(barrier, inc=1, device_id=device, device_id_type=MESH)

    def band_copy(j):
        return pltpu.make_async_remote_copy(
            src_ref=band_out.at[j],
            dst_ref=band_in.at[j],
            send_sem=band_send.at[j],
            recv_sem=band_recv.at[j],
            device_id=other,
            device_id_type=MESH,
        )

    def chain_copy(src, dst, send, recv, k, j, edge):
        return pltpu.make_async_remote_copy(
            src_ref=src.at[k, j, pl.ds(edge * EDGE, GHOST)],
            dst_ref=dst.at[k, j, edge, pl.ds(0, GHOST)],
            send_sem=send.at[k, j, edge],
            recv_sem=recv.at[k, j, edge],
            device_id=far if edge == FAR else near,
            device_id_type=MESH,
        )

    def ghost_copy(k, j, edge):
        return chain_copy(ghost_out, ghost_in, ghost_send, ghost_recv, k, j, edge)

    def back_copy(k, j, edge):
        return chain_copy(back_out, back_in, back_send, back_recv, k, j, edge)

    info_copy = pltpu.make_async_remote_copy(
        src_ref=info_out,
        dst_ref=info_in,
        send_sem=info_sems.at[0],
        recv_sem=info_sems.at[1],
        device_id=far,
        device_id_type=MESH,
    )

    x_hi, x_lo = split(states[...])

    def rotated_chunk(which, j):
        at = pl.multiple_of(which * BANDW + j * W, W)
        c_hi, c_lo = split(coefficients[:, pl.ds(at, W)])
        return fold(dot(x_hi, jnp.concatenate([c_hi, c_lo], axis=1))) + dot(x_lo, c_hi)

    for j in range(2):
        band_out[j] = rotated_chunk(1 - band, j)
        if j == 0:
            pl.semaphore_wait(barrier, 3)
        band_copy(j).start()
    for j in range(2):
        now[j] = rotated_chunk(band, j)

    list_pad[...] = jnp.full(list_pad.shape, -1, jnp.int32)
    first, second = shared[0, 0:1, :], shared[0, 1:2, :]
    list_pad[0:1, :GHOST] = jnp.where(core == 0, first, second)
    list_pad[1:2, :GHOST] = jnp.where(core == 0, second, first)
    for edge in (FAR, NEAR):
        row = list_pad[edge : edge + 1, :]
        place[edge] = hot(iota((OWN, EDGE), 0) == row[:, :EDGE])
        turn[:, :256] = jnp.broadcast_to(row.astype(F32), (W, 256))
        column = turn[:, :256].T[:EDGE]
        if edge == FAR:
            info_out[0] = column
        column = column.astype(jnp.int32)
        for at in range(0, OWN, W):
            width = min(W, OWN - at)
            pick[edge * EDGE : (edge + 1) * EDGE, at : at + width] = hot(
                iota((EDGE, width), 1) + at == column[:, :width]
            )

    turn[...] = jnp.zeros_like(turn)
    turn[:, :OWN] = jnp.broadcast_to(mass[...].reshape(1, OWN), (W, OWN))
    columns = turn[...].T[:OWN]
    mass_sq[...] = columns * columns
    mass_inv[...] = 1.0 / columns
    far_sq[...] = fold(dot(pick[:EDGE], pair(mass_sq[...])))
    info_out[1] = far_sq[...]
    info_copy.start()
    for j in range(2):
        now[j] = now[j] * columns

    edge_hi[...] = jnp.zeros_like(edge_hi)
    edge_lo[...] = jnp.zeros_like(edge_lo)
    stack[...] = jnp.zeros_like(stack)
    back_in[:, :, :, GHOST:] = jnp.zeros((DEGREE, 2, 2, EDGE - GHOST, W), F32)
    ghost_in[:, :, :, GHOST:] = jnp.zeros((DEGREE, 2, 2, EDGE - GHOST, W), F32)
    stiff_pad[...] = jnp.zeros_like(stiff_pad)
    stiff_pad[:NPE, :NPE] = stiffness[...]
    slot_pad[...] = jnp.full(slot_pad.shape, -1, jnp.int32)
    drawn = slots[...]
    is_low = (drawn >= OWN) & (drawn < OWN + GHOST)
    is_high = drawn >= OWN + GHOST
    absent = ((me == 0) & is_low) | ((me == parts - 1) & is_high)
    low_at = jnp.where(core == 0, drawn, drawn + EDGE)
    high_at = jnp.where(core == 0, drawn + (EDGE - GHOST), drawn - GHOST)
    placed = jnp.where(is_low, low_at, jnp.where(is_high, high_at, drawn))
    slot_pad[:CELLS, :NPE] = jnp.where(absent, -1, placed)
    pot_pad[...] = jnp.zeros_like(pot_pad)
    pot_pad[:CELLS, :NPE] = potential[...]

    @pl.loop(0, CELLS)
    def _(c):
        at = pl.multiple_of(c * PAD, PAD)
        row = slot_pad[pl.ds(c, 1), :]
        nodes = hot(iota((ROWS, PAD), 0) == row)
        one_hot[:, pl.ds(at, PAD)] = nodes
        diagonal = iota((PAD, PAD), 0) == iota((PAD, PAD), 1)
        cell = scale[c] * stiff_pad[...] + jnp.where(diagonal, pot_pad[pl.ds(c, 1), :], 0.0)
        stacked = jnp.concatenate(split(cell), axis=0)
        for start, size, high, low, lane in (
            (0, OWN, prod_own_hi, prod_own_lo, 0),
            (OWN, EDGE, prod_edge_hi, prod_edge_lo, 0),
            (OWN + EDGE, EDGE, prod_edge_hi, prod_edge_lo, 256),
        ):
            both = dot_nt(stacked, nodes[start : start + size])
            cols = slice(lane, lane + size)
            high[pl.ds(at, PAD), cols], low[pl.ds(at, PAD), cols] = split(both[:PAD] + both[PAD:])

    def block(rows, cols, high, low):
        left = one_hot[rows, :]
        return dot(left, high[:, cols]) + dot(left, low[:, cols])

    def own_block(at):
        end = min(at + 256, OWN)
        whole = block(slice(at, ROWS), slice(at, end), prod_own_hi, prod_own_lo)
        own_hi[at:, at:end], own_lo[at:, at:end] = split(whole)
        if end < OWN:
            flipped = whole[end - at : OWN - at].T
            own_hi[at:end, end:], own_lo[at:end, end:] = split(flipped)
        for edge in (FAR, NEAR):
            row = OWN - at + edge * EDGE
            cols = slice((edge + 1) * 256, (edge + 1) * 256 + EDGE)
            edge_hi[at:end, cols], edge_lo[at:end, cols] = split(whole[row : row + EDGE].T)

    def edge_block():
        for edge in (FAR, NEAR):
            cols = slice(edge * 256, edge * 256 + EDGE)
            to = slice((edge + 1) * 256, (edge + 1) * 256 + EDGE)
            square = block(slice(OWN, ROWS), cols, prod_edge_hi, prod_edge_lo)
            edge_hi[OWN:, to], edge_lo[OWN:, to] = split(square)

    def far_columns():
        edge_hi[:, :EDGE] = dot(own_hi[...], place[FAR]).astype(BF16)
        edge_lo[:, :EDGE] = dot(own_lo[...], place[FAR]).astype(BF16)

    def begin(j):
        band_copy(j).wait_recv()
        now[j] = now[j] + mass_cols() * band_in[j]
        ghost_out[0, j] = fold(dot(pick[...], pair(now[j])))
        ghost_copy(0, j, FAR).start()
        ghost_copy(0, j, NEAR).start()

    def mass_cols():
        return mass_sq[...] * mass_inv[...]

    def own_product(j):
        pre[j] = apply_pair(own_hi[...], own_lo[...], pair(now[j]))

    def contribute(k, j):
        for edge in (NEAR, FAR):
            ghost_copy(k, j, edge).wait_recv()
        far_ghost = ghost_in[k, j, FAR]
        if k > 0:
            far_ghost = far_ghost + COEFS[k - 1][0] * echo[j]
        stack[j, 256 : 256 + EDGE] = far_ghost
        stack[j, 512 : 512 + EDGE] = ghost_in[k, j, NEAR]
        start = 0 if k > 0 else 256
        packed = pair(stack[j, start:])
        sent = pre[j, OWN:] + apply_pair(edge_hi[OWN:, start:], edge_lo[OWN:, start:], packed)
        back_out[k, j] = sent
        back_copy(k, j, NEAR).start()
        back_copy(k, j, FAR).start()
        acc[j] = pre[j, :OWN] + apply_pair(edge_hi[:OWN, start:], edge_lo[:OWN, start:], packed)
        if k < DEGREE - 1:
            echo[j] = info_in[1] * fold(dot(same[...], pair(sent[:EDGE])))

    def settle_chip(k, j):
        back_copy(k, j, NEAR).wait_recv()
        front, past = COEFS[k]
        raw = acc[j] + fold(dot(place[NEAR], pair(back_in[k, j, NEAR])))
        current = now[j]
        following = front * (mass_sq[...] * raw - centre * current)
        if k > 0:
            following = following - past * before[j]
        packed = pair(following)
        ghost_out[k + 1, j, :EDGE] = fold(dot(pick[:EDGE], packed))
        ghost_copy(k + 1, j, FAR).start()
        before[j] = current
        now[j] = following
        pre[j] = apply_pair(own_hi[...], own_lo[...], packed)

    def settle_far(k, j):
        back_copy(k, j, FAR).wait_recv()
        change = COEFS[k][0] * far_sq[...] * back_in[k, j, FAR]
        stack[j, :EDGE] = change
        following = now[j] + fold(dot(place[FAR], pair(change)))
        ghost_out[k + 1, j, EDGE:] = fold(dot(pick[EDGE:], pair(following)))
        ghost_copy(k + 1, j, NEAR).start()
        now[j] = following

    def finish(j):
        last = DEGREE - 1
        back_copy(last, j, NEAR).wait_recv()
        raw = acc[j] + fold(dot(place[NEAR], pair(back_in[last, j, NEAR])))
        front, past = COEFS[last]
        rest = centre * now[j] + (past / front) * before[j]
        back_copy(last, j, FAR).wait_recv()
        raw = raw + fold(dot(place[FAR], pair(back_in[last, j, FAR])))
        out[:, j * W : (j + 1) * W] = mass_inv[...] * (mass_sq[...] * raw - rest)

    own_block(0)
    edge_block()
    info_copy.wait_recv()
    theirs = info_in[0]
    turn[:, :256] = jnp.concatenate([theirs, jnp.zeros((256 - EDGE, W), F32)], axis=0).T
    same[...] = hot(
        jnp.concatenate([theirs, theirs[:, : EDGE - W]], axis=1) == turn[0:1, :EDGE]
    )
    begin(0)
    own_block(256)
    own_block(512)
    own_block(768)
    far_columns()
    own_product(0)
    contribute(0, 0)
    settle_chip(0, 0)
    begin(1)
    own_product(1)
    settle_far(0, 0)
    contribute(0, 1)
    settle_chip(0, 1)
    contribute(1, 0)
    settle_chip(1, 0)
    settle_far(0, 1)
    contribute(1, 1)
    settle_chip(1, 1)
    settle_far(1, 0)
    contribute(2, 0)
    settle_far(1, 1)
    contribute(2, 1)
    finish(0)
    finish(1)

    info_copy.wait_send()
    for j in range(2):
        band_copy(j).wait_send()

    @pl.loop(0, DEGREE)
    def _(k):
        for j in range(2):
            for edge in (FAR, NEAR):
                ghost_copy(k, j, edge).wait_send()
                back_copy(k, j, edge).wait_send()


def solution(mesh):
    parts = mesh.shape["mesh"]
    vmem = pl.BlockSpec(memory_space=pltpu.VMEM)
    smem = pl.BlockSpec(memory_space=pltpu.SMEM)
    dma = pltpu.SemaphoreType.DMA

    def body(states, mass, stiffness, scale, potential, slots, shared, coefficients):
        def run(*refs):
            kernel(parts, *refs)

        filtered = pl.pallas_call(
            run,
            out_shape=jax.ShapeDtypeStruct((OWN, BANDW), F32),
            in_specs=[vmem, vmem, vmem, smem, vmem, vmem, vmem, vmem],
            out_specs=vmem,
            scratch_shapes=[
                pltpu.VMEM((PAD, PAD), F32),
                pltpu.VMEM((8, PAD), jnp.int32),
                pltpu.VMEM((8, PAD), F32),
                pltpu.VMEM((8, 256), jnp.int32),
                pltpu.VMEM((W, 896), F32),
                pltpu.VMEM((OWN, W), F32),
                pltpu.VMEM((OWN, W), F32),
                pltpu.VMEM((EDGE, W), F32),
                pltpu.VMEM((ROWS, CELLS * PAD), BF16),
                pltpu.VMEM((CELLS * PAD, OWN), BF16),
                pltpu.VMEM((CELLS * PAD, OWN), BF16),
                pltpu.VMEM((CELLS * PAD, 512), BF16),
                pltpu.VMEM((CELLS * PAD, 512), BF16),
                pltpu.VMEM((ROWS, OWN), BF16),
                pltpu.VMEM((ROWS, OWN), BF16),
                pltpu.VMEM((ROWS, 768), BF16),
                pltpu.VMEM((ROWS, 768), BF16),
                pltpu.VMEM((BOTH, OWN), BF16),
                pltpu.VMEM((2, OWN, EDGE), BF16),
                pltpu.VMEM((EDGE, EDGE), BF16),
                pltpu.VMEM((2, EDGE, W), F32),
                pltpu.VMEM((2, EDGE, W), F32),
                pltpu.VMEM((2, OWN, W), F32),
                pltpu.VMEM((2, OWN, W), F32),
                pltpu.VMEM((2, OWN, W), F32),
                pltpu.VMEM((2, OWN, W), F32),
                pltpu.VMEM((2, ROWS, W), F32),
                pltpu.VMEM((2, OWN, W), F32),
                pltpu.VMEM((2, 768, W), F32),
                pltpu.VMEM((2, EDGE, W), F32),
                pltpu.VMEM((DEGREE, 2, BOTH, W), F32),
                pltpu.VMEM((DEGREE, 2, 2, EDGE, W), F32),
                pltpu.VMEM((DEGREE, 2, BOTH, W), F32),
                pltpu.VMEM((DEGREE, 2, 2, EDGE, W), F32),
                dma((2,)),
                dma((2,)),
                dma((2,)),
                dma((DEGREE, 2, 2)),
                dma((DEGREE, 2, 2)),
                dma((DEGREE, 2, 2)),
                dma((DEGREE, 2, 2)),
            ],
            compiler_params=pltpu.CompilerParams(
                collective_id=0, has_side_effects=True, vmem_limit_bytes=56 * 2**20
            ),
        )(states, mass, stiffness, scale, potential, slots, shared, coefficients)
        return filtered * COEFS[-1][0]

    return jax.shard_map(
        body,
        mesh=mesh,
        in_specs=(
            P("mesh", "band"),
            P("mesh"),
            P(),
            P("mesh"),
            P("mesh", None),
            P("mesh", None),
            P("mesh", None, None),
            P("band", None),
        ),
        out_specs=P("mesh", "band"),
        check_vma=False,
    )
```

time: 71.5 us -> 68.5 us (0.958)
  Pallas kernels: 68.5 us -> 65.5 us
    pallas_call x1, Pallas kernels: 68.5 us -> 65.5 us  [body(): pl.pallas_call(run, out_shape=jax.ShapeDtypeStruct((OWN, BANDW), F32), in...]
where the time goes in v3:
time: 68.5 us; the launch traced here: 67.7 us
  Pallas kernels  65.5 us (96%)
  other arithmetic  2.16 us (3%)
    pallas_call x1, Pallas kernels, body(): pl.pallas_call(run, out_shape=jax.ShapeDtypeStruct((OWN, BANDW), F32), in...  65.5 us
    mul x1, other arithmetic, body(): return filtered * COEFS[-1][0]  2.16 us

profile of v3, /device:TPU:2, one launch (start us, length us, event | category | flops | bytes accessed | tf_op | source)
XLA Modules:
  0.0 67.7 jit_solution(12548769803236865819)
XLA Ops:
  0.0 65.5 %shard_map.82 = f32[864,256]{1,0:T(8,128)} custom-call(f32[864,256]{1,0:T(8,128)} %refs_0_.1, f32[864]{0:T(1024)} %refs_1_.1, f32[343,343]{1,0:T(8,128)} %refs_2_.1, f32[4]{0:T(128)} %refs_3_.1, f32[4,343]{1,0:T(4,128)} %refs_4_.1, s32[4,343]{1,0:T(4,128)} %refs_5_.1, s32[1,2,216]{2,1,0:T(2,128)} %refs_6_.1, f32[256,512]{1,0:T(8,128)} %refs_7_.1), custom_call_target="tpu_custom_call" | custom-call | tf_op jit(solution)/shard_map/pallas_call | solution.py:407
  65.5 2.2 %broadcast_multiply_fusion = f32[864,256]{1,0:T(8,128)} fusion(f32[864,256]{1,0:T(8,128)} %shard_map.82), kind=kLoop, calls=%fused_computation | loop fusion | flops 221184 | bytes 1769472 | tf_op jit(solution)/shard_map/mul | solution.py:459

commit v4 on v3

--- a/solution.py
+++ b/solution.py
@@ -12,6 +12,7 @@
 OWN = 864
 GHOST = 216
 EDGE = 224
+HALF = OWN // 2
 BOTH = 2 * EDGE
 ROWS = OWN + BOTH
 NPE = 343
@@ -108,6 +109,8 @@
     pick,
     place,
     same,
+    order,
+    back_order,
     info_out,
     info_in,
     band_out,
@@ -117,6 +120,8 @@
     pre,
     acc,
     stack,
+    stack_pair,
+    own_pair,
     echo,
     ghost_out,
     ghost_in,
@@ -141,12 +146,13 @@
     for device in (other, far, near):
         pl.semaphore_signal(barrier, inc=1, device_id=device, device_id_type=MESH)
 
-    def band_copy(j):
+    def band_copy(part):
+        piece = (0,) if part == 0 else (1, pl.ds((part - 1) * HALF, HALF))
         return pltpu.make_async_remote_copy(
-            src_ref=band_out.at[j],
-            dst_ref=band_in.at[j],
-            send_sem=band_send.at[j],
-            recv_sem=band_recv.at[j],
+            src_ref=band_out.at[piece],
+            dst_ref=band_in.at[piece],
+            send_sem=band_send.at[part],
+            recv_sem=band_recv.at[part],
             device_id=other,
             device_id_type=MESH,
         )
@@ -183,22 +189,22 @@
         c_hi, c_lo = split(coefficients[:, pl.ds(at, W)])
         return fold(dot(x_hi, jnp.concatenate([c_hi, c_lo], axis=1))) + dot(x_lo, c_hi)
 
-    for j in range(2):
-        band_out[j] = rotated_chunk(1 - band, j)
-        if j == 0:
-            pl.semaphore_wait(barrier, 3)
-        band_copy(j).start()
-    for j in range(2):
-        now[j] = rotated_chunk(band, j)
+    band_out[0] = rotated_chunk(1 - band, 0)
+    pl.semaphore_wait(barrier, 3)
+    band_copy(0).start()
 
     list_pad[...] = jnp.full(list_pad.shape, -1, jnp.int32)
     first, second = shared[0, 0:1, :], shared[0, 1:2, :]
     list_pad[0:1, :GHOST] = jnp.where(core == 0, first, second)
     list_pad[1:2, :GHOST] = jnp.where(core == 0, second, first)
+
+    def along_rows(row, length):
+        turn[:, :length] = jnp.broadcast_to(row.astype(F32), (W, length))
+
     for edge in (FAR, NEAR):
         row = list_pad[edge : edge + 1, :]
         place[edge] = hot(iota((OWN, EDGE), 0) == row[:, :EDGE])
-        turn[:, :256] = jnp.broadcast_to(row.astype(F32), (W, 256))
+        along_rows(row, 256)
         column = turn[:, :256].T[:EDGE]
         if edge == FAR:
             info_out[0] = column
@@ -208,6 +214,29 @@
             pick[edge * EDGE : (edge + 1) * EDGE, at : at + width] = hot(
                 iota((EDGE, width), 1) + at == column[:, :width]
             )
+
+    counts = dot(jnp.ones((16, BOTH), BF16), pick[...])
+    is_shared = counts > 0.5
+    ahead = dot(hot(is_shared), hot(iota((OWN, OWN), 0) < iota((OWN, OWN), 1)))[0:1]
+    is_shared = is_shared[0:1]
+    total = jnp.sum(jnp.where(is_shared, 1.0, 0.0), axis=1, keepdims=True)
+    here = lax.broadcasted_iota(jnp.int32, (1, OWN), 1).astype(F32)
+    rank = jnp.where(is_shared, ahead, total + here - ahead)
+    order[...] = hot(iota((OWN, OWN), 0) == rank.astype(jnp.int32))
+    band_out[1] = fold(dot(order[...], pair(rotated_chunk(1 - band, 1))))
+    for part in (1, 2):
+        band_copy(part).start()
+    turn[:, OWN:] = jnp.zeros((W, 896 - OWN), F32)
+    along_rows(rank, OWN)
+    column = turn[...].T[:OWN].astype(jnp.int32)
+    for half in range(2):
+        for at in range(0, HALF, W):
+            width = min(W, HALF - at)
+            back_order[half, :, at : at + width] = hot(
+                iota((OWN, width), 1) + (half * HALF + at) == column[:, :width]
+            )
+    for j in range(2):
+        now[j] = rotated_chunk(band, j)
 
     turn[...] = jnp.zeros_like(turn)
     turn[:, :OWN] = jnp.broadcast_to(mass[...].reshape(1, OWN), (W, OWN))
@@ -263,15 +292,19 @@
 
     def own_block(at):
         end = min(at + 256, OWN)
-        whole = block(slice(at, ROWS), slice(at, end), prod_own_hi, prod_own_lo)
-        own_hi[at:, at:end], own_lo[at:, at:end] = split(whole)
+        whole = block(slice(at, OWN), slice(at, end), prod_own_hi, prod_own_lo)
+        own_hi[at:OWN, at:end], own_lo[at:OWN, at:end] = split(whole)
         if end < OWN:
-            flipped = whole[end - at : OWN - at].T
-            own_hi[at:end, end:], own_lo[at:end, end:] = split(flipped)
+            own_hi[at:end, end:], own_lo[at:end, end:] = split(whole[end - at :].T)
+
+    def edge_rows(at):
+        end = min(at + 256, OWN)
+        whole = block(slice(OWN, ROWS), slice(at, end), prod_own_hi, prod_own_lo)
+        own_hi[OWN:, at:end], own_lo[OWN:, at:end] = split(whole)
         for edge in (FAR, NEAR):
-            row = OWN - at + edge * EDGE
             cols = slice((edge + 1) * 256, (edge + 1) * 256 + EDGE)
-            edge_hi[at:end, cols], edge_lo[at:end, cols] = split(whole[row : row + EDGE].T)
+            flipped = whole[edge * EDGE : (edge + 1) * EDGE].T
+            edge_hi[at:end, cols], edge_lo[at:end, cols] = split(flipped)
 
     def edge_block():
         for edge in (FAR, NEAR):
@@ -285,17 +318,30 @@
         edge_lo[:, :EDGE] = dot(own_lo[...], place[FAR]).astype(BF16)
 
     def begin(j):
-        band_copy(j).wait_recv()
-        now[j] = now[j] + mass_cols() * band_in[j]
         ghost_out[0, j] = fold(dot(pick[...], pair(now[j])))
         ghost_copy(0, j, FAR).start()
         ghost_copy(0, j, NEAR).start()
 
+    def begin_whole():
+        band_copy(0).wait_recv()
+        now[0] = now[0] + mass_cols() * band_in[0]
+        own_pair[0] = pair(now[0])
+        begin(0)
+
+    def begin_half(half):
+        band_copy(1 + half).wait_recv()
+        arrived = pair(band_in[1, half * HALF : (half + 1) * HALF])
+        now[1] = now[1] + mass_cols() * fold(dot(back_order[half], arrived))
+        if half == 0:
+            begin(1)
+        else:
+            own_pair[1] = pair(now[1])
+
     def mass_cols():
         return mass_sq[...] * mass_inv[...]
 
     def own_product(j):
-        pre[j] = apply_pair(own_hi[...], own_lo[...], pair(now[j]))
+        pre[j] = apply_pair(own_hi[...], own_lo[...], own_pair[j])
 
     def contribute(k, j):
         for edge in (NEAR, FAR):
@@ -307,13 +353,20 @@
         stack[j, 512 : 512 + EDGE] = ghost_in[k, j, NEAR]
         start = 0 if k > 0 else 256
         packed = pair(stack[j, start:])
-        sent = pre[j, OWN:] + apply_pair(edge_hi[OWN:, start:], edge_lo[OWN:, start:], packed)
-        back_out[k, j] = sent
+        stack_pair[j, start:] = packed
+        back_out[k, j] = pre[j, OWN:] + apply_pair(
+            edge_hi[OWN:, start:], edge_lo[OWN:, start:], packed
+        )
         back_copy(k, j, NEAR).start()
         back_copy(k, j, FAR).start()
-        acc[j] = pre[j, :OWN] + apply_pair(edge_hi[:OWN, start:], edge_lo[:OWN, start:], packed)
+
+    def gather_own(k, j):
+        start = 0 if k > 0 else 256
+        acc[j] = pre[j, :OWN] + apply_pair(
+            edge_hi[:OWN, start:], edge_lo[:OWN, start:], stack_pair[j, start:]
+        )
         if k < DEGREE - 1:
-            echo[j] = info_in[1] * fold(dot(same[...], pair(sent[:EDGE])))
+            echo[j] = info_in[1] * fold(dot(same[...], pair(back_out[k, j, :EDGE])))
 
     def settle_chip(k, j):
         back_copy(k, j, NEAR).wait_recv()
@@ -324,11 +377,11 @@
         if k > 0:
             following = following - past * before[j]
         packed = pair(following)
+        own_pair[j] = packed
         ghost_out[k + 1, j, :EDGE] = fold(dot(pick[:EDGE], packed))
         ghost_copy(k + 1, j, FAR).start()
         before[j] = current
         now[j] = following
-        pre[j] = apply_pair(own_hi[...], own_lo[...], packed)
 
     def settle_far(k, j):
         back_copy(k, j, FAR).wait_recv()
@@ -350,6 +403,12 @@
         out[:, j * W : (j + 1) * W] = mass_inv[...] * (mass_sq[...] * raw - rest)
 
     own_block(0)
+    own_block(256)
+    own_block(512)
+    own_block(768)
+    begin_whole()
+    for at in range(0, OWN, 256):
+        edge_rows(at)
     edge_block()
     info_copy.wait_recv()
     theirs = info_in[0]
@@ -357,34 +416,41 @@
     same[...] = hot(
         jnp.concatenate([theirs, theirs[:, : EDGE - W]], axis=1) == turn[0:1, :EDGE]
     )
-    begin(0)
-    own_block(256)
-    own_block(512)
-    own_block(768)
+    own_product(0)
+    begin_half(0)
+    contribute(0, 0)
+    gather_own(0, 0)
+    settle_chip(0, 0)
+    own_product(0)
+    begin_half(1)
+    own_product(1)
+    contribute(0, 1)
+    settle_far(0, 0)
+    gather_own(0, 1)
+    settle_chip(0, 1)
+    own_product(1)
     far_columns()
+    contribute(1, 0)
+    settle_far(0, 1)
+    gather_own(1, 0)
+    settle_chip(1, 0)
+    contribute(1, 1)
+    gather_own(1, 1)
+    settle_chip(1, 1)
+    own_product(1)
+    settle_far(1, 0)
     own_product(0)
-    contribute(0, 0)
-    settle_chip(0, 0)
-    begin(1)
-    own_product(1)
-    settle_far(0, 0)
-    contribute(0, 1)
-    settle_chip(0, 1)
-    contribute(1, 0)
-    settle_chip(1, 0)
-    settle_far(0, 1)
-    contribute(1, 1)
-    settle_chip(1, 1)
-    settle_far(1, 0)
     contribute(2, 0)
     settle_far(1, 1)
     contribute(2, 1)
+    gather_own(2, 1)
+    gather_own(2, 0)
     finish(0)
     finish(1)
 
     info_copy.wait_send()
-    for j in range(2):
-        band_copy(j).wait_send()
+    for part in range(3):
+        band_copy(part).wait_send()
 
     @pl.loop(0, DEGREE)
     def _(k):
@@ -430,6 +496,8 @@
                 pltpu.VMEM((BOTH, OWN), BF16),
                 pltpu.VMEM((2, OWN, EDGE), BF16),
                 pltpu.VMEM((EDGE, EDGE), BF16),
+                pltpu.VMEM((OWN, OWN), BF16),
+                pltpu.VMEM((2, OWN, HALF), BF16),
                 pltpu.VMEM((2, EDGE, W), F32),
                 pltpu.VMEM((2, EDGE, W), F32),
                 pltpu.VMEM((2, OWN, W), F32),
@@ -439,21 +507,23 @@
                 pltpu.VMEM((2, ROWS, W), F32),
                 pltpu.VMEM((2, OWN, W), F32),
                 pltpu.VMEM((2, 768, W), F32),
+                pltpu.VMEM((2, 768, 2 * W), BF16),
+                pltpu.VMEM((2, OWN, 2 * W), BF16),
                 pltpu.VMEM((2, EDGE, W), F32),
                 pltpu.VMEM((DEGREE, 2, BOTH, W), F32),
                 pltpu.VMEM((DEGREE, 2, 2, EDGE, W), F32),
                 pltpu.VMEM((DEGREE, 2, BOTH, W), F32),
                 pltpu.VMEM((DEGREE, 2, 2, EDGE, W), F32),
                 dma((2,)),
-                dma((2,)),
-                dma((2,)),
+                dma((3,)),
+                dma((3,)),
                 dma((DEGREE, 2, 2)),
                 dma((DEGREE, 2, 2)),
                 dma((DEGREE, 2, 2)),
                 dma((DEGREE, 2, 2)),
             ],
             compiler_params=pltpu.CompilerParams(
-                collective_id=0, has_side_effects=True, vmem_limit_bytes=56 * 2**20
+                collective_id=0, has_side_effects=True, vmem_limit_bytes=46 * 2**20
             ),
         )(states, mass, stiffness, scale, potential, slots, shared, coefficients)
         return filtered * COEFS[-1][0]

time: 68.5 us -> 67 us (0.978)
  Pallas kernels: 65.5 us -> 58.3 us
  local copies, waits for them, and re-layouts: 0 us -> 6.65 us
  other arithmetic: 2.16 us -> 1 us
    pallas_call x1, Pallas kernels: 65.5 us -> 58.3 us  [body(): pl.pallas_call(run, out_shape=jax.ShapeDtypeStruct((OWN, BANDW), F32), in...]
    unnamed x0 -> x16, local copies, waits for them, and re-layouts: none -> 6.65 us
    mul x1, other arithmetic: 2.16 us -> 1 us  [body(): return filtered * COEFS[-1][0]]
where the time goes in v4:
time: 67 us; the launch traced here: 66 us
  Pallas kernels  58.3 us (87%)
  local copies, waits for them, and re-layouts  6.65 us (10%)
  other arithmetic  1 us (1%)
    pallas_call x1, Pallas kernels, body(): pl.pallas_call(run, out_shape=jax.ShapeDtypeStruct((OWN, BANDW), F32), in...  58.3 us
    unnamed x16, local copies, waits for them, and re-layouts  6.65 us

profile of v4, /device:TPU:2, one launch (start us, length us, event | category | flops | bytes accessed | tf_op | source)
XLA Modules:
  0.0 66.0 jit_solution(8342755317298407041)
XLA Ops:
  0.0 0.0 copy-start
  0.0 1.2 %copy-done = f32[864,256]{1,0:T(8,128)S(1)} copy-done((f32[864,256]{1,0:T(8,128)S(1)}, f32[864,256]{1,0:T(8,128)}, u32[]{:S(2)}) %copy-start) | copy-done | bytes 884760
  1.2 0.0 copy-start.1
  1.2 1.0 %copy-done.1 = f32[343,343]{1,0:T(8,128)S(1)} copy-done((f32[343,343]{1,0:T(8,128)S(1)}, f32[343,343]{1,0:T(8,128)}, u32[]{:S(2)}) %copy-start.1) | copy-done | bytes 470620
  2.2 0.0 copy-start.2
  2.2 1.0 %copy-done.2 = f32[256,512]{1,0:T(8,128)S(1)} copy-done((f32[256,512]{1,0:T(8,128)S(1)}, f32[256,512]{1,0:T(8,128)}, u32[]{:S(2)}) %copy-start.2) | copy-done | bytes 524312
  3.3 0.0 copy-start.3
  3.3 0.7 %copy-done.3 = f32[4,343]{1,0:T(4,128)S(1)} copy-done((f32[4,343]{1,0:T(4,128)S(1)}, f32[4,343]{1,0:T(4,128)}, u32[]{:S(2)}) %copy-start.3) | copy-done | bytes 5512
  3.9 0.0 copy-start.4
  3.9 0.7 %copy-done.4 = s32[4,343]{1,0:T(4,128)S(1)} copy-done((s32[4,343]{1,0:T(4,128)S(1)}, s32[4,343]{1,0:T(4,128)}, u32[]{:S(2)}) %copy-start.4) | copy-done | bytes 5512
  4.6 0.0 copy-start.5
  4.6 0.7 %copy-done.5 = f32[864]{0:T(1024)S(1)} copy-done((f32[864]{0:T(1024)S(1)}, f32[864]{0:T(1024)}, u32[]{:S(2)}) %copy-start.5) | copy-done | bytes 3480
  5.3 0.0 copy-start.6
  5.3 0.7 %copy-done.6 = s32[1,2,216]{2,1,0:T(2,128)S(1)} copy-done((s32[1,2,216]{2,1,0:T(2,128)S(1)}, s32[1,2,216]{2,1,0:T(2,128)}, u32[]{:S(2)}) %copy-start.6) | copy-done | bytes 1752
  6.0 0.0 copy-start.7
  6.0 0.7 copy-done.7
  6.7 58.3 %shard_map.82 = f32[864,256]{1,0:T(8,128)S(1)} custom-call(f32[864,256]{1,0:T(8,128)S(1)} %copy-done, f32[864]{0:T(1024)S(1)} %copy-done.5, f32[343,343]{1,0:T(8,128)S(1)} %copy-done.1, f32[4]{0:T(128)S(1)} %copy-done.7, f32[4,343]{1,0:T(4,128)S(1)} %copy-done.3, s32[4,343]{1,0:T(4,128)S(1)} %copy-done.4, s32[1,2,216]{2,1,0:T(2,128)S(1)} %copy-done.6, ...), custom_call_target="tpu_custom_call" | custom-call | tf_op jit(solution)/shard_map/pallas_call | solution.py:473
  65.0 1.0 %broadcast_multiply_fusion = f32[864,256]{1,0:T(8,128)} fusion(f32[864,256]{1,0:T(8,128)S(1)} %shard_map.82), kind=kLoop, calls=%fused_computation | loop fusion | flops 221184 | bytes 1769472 | tf_op jit(solution)/shard_map/mul | solution.py:529
Async XLA Ops:
  0.0 1.2 %copy-start = (f32[864,256]{1,0:T(8,128)S(1)}, f32[864,256]{1,0:T(8,128)}, u32[]{:S(2)}) copy-start(f32[864,256]{1,0:T(8,128)} %refs_0_.1) | copy-start | bytes 2654212
  1.2 1.0 %copy-start.1 = (f32[343,343]{1,0:T(8,128)S(1)}, f32[343,343]{1,0:T(8,128)}, u32[]{:S(2)}) copy-start(f32[343,343]{1,0:T(8,128)} %refs_2_.1) | copy-start | bytes 1411792
  2.2 1.0 %copy-start.2 = (f32[256,512]{1,0:T(8,128)S(1)}, f32[256,512]{1,0:T(8,128)}, u32[]{:S(2)}) copy-start(f32[256,512]{1,0:T(8,128)} %refs_7_.1) | copy-start | bytes 1572868
  3.3 0.7 %copy-start.3 = (f32[4,343]{1,0:T(4,128)S(1)}, f32[4,343]{1,0:T(4,128)}, u32[]{:S(2)}) copy-start(f32[4,343]{1,0:T(4,128)} %refs_4_.1) | copy-start | bytes 16468
  3.9 0.7 %copy-start.4 = (s32[4,343]{1,0:T(4,128)S(1)}, s32[4,343]{1,0:T(4,128)}, u32[]{:S(2)}) copy-start(s32[4,343]{1,0:T(4,128)} %refs_5_.1) | copy-start | bytes 16468
  4.6 0.7 %copy-start.5 = (f32[864]{0:T(1024)S(1)}, f32[864]{0:T(1024)}, u32[]{:S(2)}) copy-start(f32[864]{0:T(1024)} %refs_1_.1) | copy-start | bytes 10372
  5.3 0.7 %copy-start.6 = (s32[1,2,216]{2,1,0:T(2,128)S(1)}, s32[1,2,216]{2,1,0:T(2,128)}, u32[]{:S(2)}) copy-start(s32[1,2,216]{2,1,0:T(2,128)} %refs_6_.1) | copy-start | bytes 5188
  6.0 0.7 copy-start.7

commit v5 on v4

--- a/solution.py
+++ b/solution.py
@@ -80,15 +80,23 @@
 
 def kernel(
     parts,
+    states_at,
+    mass_at,
+    stiffness_at,
+    scale,
+    potential_at,
+    slots_at,
+    shared_at,
+    coefficients_at,
+    out,
     states,
+    coefficients,
+    shared,
     mass,
     stiffness,
-    scale,
     potential,
     slots,
-    shared,
-    coefficients,
-    out,
+    load_sems,
     stiff_pad,
     slot_pad,
     pot_pad,
@@ -137,6 +145,23 @@
 ):
     me = lax.axis_index("mesh")
     band = lax.axis_index("band")
+    loads = [
+        pltpu.make_async_copy(source, target, load_sems.at[at])
+        for at, (source, target) in enumerate(
+            (
+                (states_at, states),
+                (coefficients_at, coefficients),
+                (shared_at, shared),
+                (mass_at, mass),
+                (stiffness_at, stiffness),
+                (potential_at, potential),
+                (slots_at, slots),
+            )
+        )
+    ]
+    for load in loads:
+        load.start()
+
     core = lax.rem(me, 2)
     near = (me + 1 - 2 * core, band)
     far = (lax.rem(me + parts - 1 + 2 * core, parts), band)
@@ -182,6 +207,8 @@
         device_id_type=MESH,
     )
 
+    loads[0].wait()
+    loads[1].wait()
     x_hi, x_lo = split(states[...])
 
     def rotated_chunk(which, j):
@@ -193,6 +220,8 @@
     pl.semaphore_wait(barrier, 3)
     band_copy(0).start()
 
+    for load in loads[2:]:
+        load.wait()
     list_pad[...] = jnp.full(list_pad.shape, -1, jnp.int32)
     first, second = shared[0, 0:1, :], shared[0, 1:2, :]
     list_pad[0:1, :GHOST] = jnp.where(core == 0, first, second)
@@ -464,6 +493,7 @@
     parts = mesh.shape["mesh"]
     vmem = pl.BlockSpec(memory_space=pltpu.VMEM)
     smem = pl.BlockSpec(memory_space=pltpu.SMEM)
+    hbm = pl.BlockSpec(memory_space=pltpu.HBM)
     dma = pltpu.SemaphoreType.DMA
 
     def body(states, mass, stiffness, scale, potential, slots, shared, coefficients):
@@ -473,9 +503,17 @@
         filtered = pl.pallas_call(
             run,
             out_shape=jax.ShapeDtypeStruct((OWN, BANDW), F32),
-            in_specs=[vmem, vmem, vmem, smem, vmem, vmem, vmem, vmem],
+            in_specs=[hbm, hbm, hbm, smem, hbm, hbm, hbm, hbm],
             out_specs=vmem,
             scratch_shapes=[
+                pltpu.VMEM(states.shape, F32),
+                pltpu.VMEM(coefficients.shape, F32),
+                pltpu.VMEM(shared.shape, jnp.int32),
+                pltpu.VMEM(mass.shape, F32),
+                pltpu.VMEM(stiffness.shape, F32),
+                pltpu.VMEM(potential.shape, F32),
+                pltpu.VMEM(slots.shape, jnp.int32),
+                dma((7,)),
                 pltpu.VMEM((PAD, PAD), F32),
                 pltpu.VMEM((8, PAD), jnp.int32),
                 pltpu.VMEM((8, PAD), F32),
@@ -523,7 +561,7 @@
                 dma((DEGREE, 2, 2)),
             ],
             compiler_params=pltpu.CompilerParams(
-                collective_id=0, has_side_effects=True, vmem_limit_bytes=46 * 2**20
+                collective_id=0, has_side_effects=True, vmem_limit_bytes=56 * 2**20
             ),
         )(states, mass, stiffness, scale, potential, slots, shared, coefficients)
         return filtered * COEFS[-1][0]

time: 67 us -> 62.4 us (0.931)
  local copies, waits for them, and re-layouts: 6.65 us -> 0 us
  Pallas kernels: 58.3 us -> 59.5 us
  other arithmetic: 1 us -> 2.16 us
    unnamed x16 -> x0, local copies, waits for them, and re-layouts: 6.65 us -> none
    mul x1, other arithmetic: 1 us -> 2.16 us  [body(): return filtered * COEFS[-1][0]]
    pallas_call x1, Pallas kernels: 58.3 us -> 59.5 us  [body(): pl.pallas_call(run, out_shape=jax.ShapeDtypeStruct((OWN, BANDW), F32), in...]
where the time goes in v5:
time: 62.4 us; the launch traced here: 61.6 us
  Pallas kernels  59.5 us (95%)
  other arithmetic  2.16 us (3%)
    pallas_call x1, Pallas kernels, body(): pl.pallas_call(run, out_shape=jax.ShapeDtypeStruct((OWN, BANDW), F32), in...  59.5 us
    mul x1, other arithmetic, body(): return filtered * COEFS[-1][0]  2.16 us

profile of v5, /device:TPU:2, one launch (start us, length us, event | category | flops | bytes accessed | tf_op | source)
XLA Modules:
  0.0 61.6 jit_solution(5678013676447230839)
XLA Ops:
  0.0 59.5 %shard_map.82 = f32[864,256]{1,0:T(8,128)} custom-call(f32[864,256]{1,0:T(8,128)} %refs_0_.1, f32[864]{0:T(1024)} %refs_1_.1, f32[343,343]{1,0:T(8,128)} %refs_2_.1, f32[4]{0:T(128)} %refs_3_.1, f32[4,343]{1,0:T(4,128)} %refs_4_.1, s32[4,343]{1,0:T(4,128)} %refs_5_.1, s32[1,2,216]{2,1,0:T(2,128)} %refs_6_.1, f32[256,512]{1,0:T(8,128)} %refs_7_.1), custom_call_target="tpu_custom_call" | custom-call | tf_op jit(solution)/shard_map/pallas_call | solution.py:503
  59.5 2.2 %broadcast_multiply_fusion = f32[864,256]{1,0:T(8,128)} fusion(f32[864,256]{1,0:T(8,128)} %shard_map.82), kind=kLoop, calls=%fused_computation | loop fusion | flops 221184 | bytes 1769472 | tf_op jit(solution)/shard_map/mul | solution.py:567

commit v6 on v5

--- a/solution.py
+++ b/solution.py
@@ -17,6 +17,7 @@
 ROWS = OWN + BOTH
 NPE = 343
 PAD = 384
+KEEP = 352
 CELLS = 4
 W = 128
 BANDW = 256
@@ -303,8 +304,8 @@
         row = slot_pad[pl.ds(c, 1), :]
         nodes = hot(iota((ROWS, PAD), 0) == row)
         one_hot[:, pl.ds(at, PAD)] = nodes
-        diagonal = iota((PAD, PAD), 0) == iota((PAD, PAD), 1)
-        cell = scale[c] * stiff_pad[...] + jnp.where(diagonal, pot_pad[pl.ds(c, 1), :], 0.0)
+        diagonal = iota((KEEP, PAD), 0) == iota((KEEP, PAD), 1)
+        cell = scale[c] * stiff_pad[:KEEP] + jnp.where(diagonal, pot_pad[pl.ds(c, 1), :], 0.0)
         stacked = jnp.concatenate(split(cell), axis=0)
         for start, size, high, low, lane in (
             (0, OWN, prod_own_hi, prod_own_lo, 0),
@@ -313,7 +314,11 @@
         ):
             both = dot_nt(stacked, nodes[start : start + size])
             cols = slice(lane, lane + size)
-            high[pl.ds(at, PAD), cols], low[pl.ds(at, PAD), cols] = split(both[:PAD] + both[PAD:])
+            total_rows = both[:KEEP] + both[KEEP:]
+            high[pl.ds(at, KEEP), cols], low[pl.ds(at, KEEP), cols] = split(total_rows)
+            spare = pl.ds(pl.multiple_of(at + KEEP, 32), PAD - KEEP)
+            for to in (high, low):
+                to[spare, cols] = jnp.zeros((PAD - KEEP, size), BF16)
 
     def block(rows, cols, high, low):
         left = one_hot[rows, :]
@@ -431,34 +436,32 @@
         raw = raw + fold(dot(place[FAR], pair(back_in[last, j, FAR])))
         out[:, j * W : (j + 1) * W] = mass_inv[...] * (mass_sq[...] * raw - rest)
 
-    own_block(0)
-    own_block(256)
-    own_block(512)
-    own_block(768)
-    begin_whole()
     for at in range(0, OWN, 256):
         edge_rows(at)
     edge_block()
+    for at in range(0, OWN, 256):
+        own_block(at)
+    begin_whole()
+    own_product(0)
+    far_columns()
     info_copy.wait_recv()
     theirs = info_in[0]
     turn[:, :256] = jnp.concatenate([theirs, jnp.zeros((256 - EDGE, W), F32)], axis=0).T
     same[...] = hot(
         jnp.concatenate([theirs, theirs[:, : EDGE - W]], axis=1) == turn[0:1, :EDGE]
     )
-    own_product(0)
     begin_half(0)
     contribute(0, 0)
     gather_own(0, 0)
     settle_chip(0, 0)
-    own_product(0)
     begin_half(1)
     own_product(1)
     contribute(0, 1)
+    gather_own(0, 1)
     settle_far(0, 0)
-    gather_own(0, 1)
     settle_chip(0, 1)
+    own_product(0)
     own_product(1)
-    far_columns()
     contribute(1, 0)
     settle_far(0, 1)
     gather_own(1, 0)
@@ -466,11 +469,11 @@
     contribute(1, 1)
     gather_own(1, 1)
     settle_chip(1, 1)
-    own_product(1)
     settle_far(1, 0)
     own_product(0)
     contribute(2, 0)
     settle_far(1, 1)
+    own_product(1)
     contribute(2, 1)
     gather_own(2, 1)
     gather_own(2, 0)

time: 62.4 us -> 63.5 us (1.018)
  Pallas kernels: 59.5 us -> 60.6 us
    pallas_call x1, Pallas kernels: 59.5 us -> 60.6 us  [body(): pl.pallas_call(run, out_shape=jax.ShapeDtypeStruct((OWN, BANDW), F32), in...]
where the time goes in v6:
time: 63.5 us; the launch traced here: 62.8 us
  Pallas kernels  60.6 us (95%)
  other arithmetic  2.16 us (3%)
    pallas_call x1, Pallas kernels, body(): pl.pallas_call(run, out_shape=jax.ShapeDtypeStruct((OWN, BANDW), F32), in...  60.6 us
    mul x1, other arithmetic, body(): return filtered * COEFS[-1][0]  2.16 us

profile of v6, /device:TPU:2, one launch (start us, length us, event | category | flops | bytes accessed | tf_op | source)
XLA Modules:
  0.0 62.8 jit_solution(11101852931018409202)
XLA Ops:
  0.0 60.6 %shard_map.82 = f32[864,256]{1,0:T(8,128)} custom-call(f32[864,256]{1,0:T(8,128)} %refs_0_.1, f32[864]{0:T(1024)} %refs_1_.1, f32[343,343]{1,0:T(8,128)} %refs_2_.1, f32[4]{0:T(128)} %refs_3_.1, f32[4,343]{1,0:T(4,128)} %refs_4_.1, s32[4,343]{1,0:T(4,128)} %refs_5_.1, s32[1,2,216]{2,1,0:T(2,128)} %refs_6_.1, f32[256,512]{1,0:T(8,128)} %refs_7_.1), custom_call_target="tpu_custom_call" | custom-call | tf_op jit(solution)/shard_map/pallas_call | solution.py:506
  60.6 2.2 %broadcast_multiply_fusion = f32[864,256]{1,0:T(8,128)} fusion(f32[864,256]{1,0:T(8,128)} %shard_map.82), kind=kLoop, calls=%fused_computation | loop fusion | flops 221184 | bytes 1769472 | tf_op jit(solution)/shard_map/mul | solution.py:570

commit v7 on v6

--- a/solution.py
+++ b/solution.py
@@ -454,13 +454,13 @@
     contribute(0, 0)
     gather_own(0, 0)
     settle_chip(0, 0)
+    own_product(0)
     begin_half(1)
     own_product(1)
     contribute(0, 1)
+    settle_far(0, 0)
     gather_own(0, 1)
-    settle_far(0, 0)
     settle_chip(0, 1)
-    own_product(0)
     own_product(1)
     contribute(1, 0)
     settle_far(0, 1)
@@ -469,11 +469,11 @@
     contribute(1, 1)
     gather_own(1, 1)
     settle_chip(1, 1)
+    own_product(1)
     settle_far(1, 0)
     own_product(0)
     contribute(2, 0)
     settle_far(1, 1)
-    own_product(1)
     contribute(2, 1)
     gather_own(2, 1)
     gather_own(2, 0)

time: 63.5 us -> 63.5 us (level)
  no operation moved by 1% of the time
where the time goes in v7:
time: 63.5 us; the launch traced here: 62.8 us
  Pallas kernels  60.7 us (96%)
  other arithmetic  2.16 us (3%)
    pallas_call x1, Pallas kernels, body(): pl.pallas_call(run, out_shape=jax.ShapeDtypeStruct((OWN, BANDW), F32), in...  60.7 us
    mul x1, other arithmetic, body(): return filtered * COEFS[-1][0]  2.16 us

profile of v7, /device:TPU:2, one launch (start us, length us, event | category | flops | bytes accessed | tf_op | source)
XLA Modules:
  0.0 62.8 jit_solution(16951885799227314026)
XLA Ops:
  0.0 60.7 %shard_map.82 = f32[864,256]{1,0:T(8,128)} custom-call(f32[864,256]{1,0:T(8,128)} %refs_0_.1, f32[864]{0:T(1024)} %refs_1_.1, f32[343,343]{1,0:T(8,128)} %refs_2_.1, f32[4]{0:T(128)} %refs_3_.1, f32[4,343]{1,0:T(4,128)} %refs_4_.1, s32[4,343]{1,0:T(4,128)} %refs_5_.1, s32[1,2,216]{2,1,0:T(2,128)} %refs_6_.1, f32[256,512]{1,0:T(8,128)} %refs_7_.1), custom_call_target="tpu_custom_call" | custom-call | tf_op jit(solution)/shard_map/pallas_call | solution.py:506
  60.7 2.2 %broadcast_multiply_fusion = f32[864,256]{1,0:T(8,128)} fusion(f32[864,256]{1,0:T(8,128)} %shard_map.82), kind=kLoop, calls=%fused_computation | loop fusion | flops 221184 | bytes 1769472 | tf_op jit(solution)/shard_map/mul | solution.py:570

commit v8 on v5

--- a/solution.py
+++ b/solution.py
@@ -342,9 +342,9 @@
             square = block(slice(OWN, ROWS), cols, prod_edge_hi, prod_edge_lo)
             edge_hi[OWN:, to], edge_lo[OWN:, to] = split(square)
 
-    def far_columns():
-        edge_hi[:, :EDGE] = dot(own_hi[...], place[FAR]).astype(BF16)
-        edge_lo[:, :EDGE] = dot(own_lo[...], place[FAR]).astype(BF16)
+    def far_columns(rows):
+        edge_hi[rows, :EDGE] = dot(own_hi[rows, :], place[FAR]).astype(BF16)
+        edge_lo[rows, :EDGE] = dot(own_lo[rows, :], place[FAR]).astype(BF16)
 
     def begin(j):
         ghost_out[0, j] = fold(dot(pick[...], pair(now[j])))
@@ -435,6 +435,7 @@
     own_block(256)
     own_block(512)
     own_block(768)
+    far_columns(slice(0, OWN))
     begin_whole()
     for at in range(0, OWN, 256):
         edge_rows(at)
@@ -458,7 +459,7 @@
     gather_own(0, 1)
     settle_chip(0, 1)
     own_product(1)
-    far_columns()
+    far_columns(slice(OWN, ROWS))
     contribute(1, 0)
     settle_far(0, 1)
     gather_own(1, 0)

time: 62.4 us -> 62.4 us (level)
  no operation moved by 1% of the time
where the time goes in v8:
time: 62.4 us; the launch traced here: 62.1 us
  Pallas kernels  60 us (96%)
  other arithmetic  2.16 us (3%)
    pallas_call x1, Pallas kernels, body(): pl.pallas_call(run, out_shape=jax.ShapeDtypeStruct((OWN, BANDW), F32), in...  60 us
    mul x1, other arithmetic, body(): return filtered * COEFS[-1][0]  2.16 us

profile of v8, /device:TPU:2, one launch (start us, length us, event | category | flops | bytes accessed | tf_op | source)
XLA Modules:
  0.0 62.1 jit_solution(2692131491260504238)
XLA Ops:
  0.0 60.0 %shard_map.82 = f32[864,256]{1,0:T(8,128)} custom-call(f32[864,256]{1,0:T(8,128)} %refs_0_.1, f32[864]{0:T(1024)} %refs_1_.1, f32[343,343]{1,0:T(8,128)} %refs_2_.1, f32[4]{0:T(128)} %refs_3_.1, f32[4,343]{1,0:T(4,128)} %refs_4_.1, s32[4,343]{1,0:T(4,128)} %refs_5_.1, s32[1,2,216]{2,1,0:T(2,128)} %refs_6_.1, f32[256,512]{1,0:T(8,128)} %refs_7_.1), custom_call_target="tpu_custom_call" | custom-call | tf_op jit(solution)/shard_map/pallas_call | solution.py:504
  60.0 2.2 %broadcast_multiply_fusion = f32[864,256]{1,0:T(8,128)} fusion(f32[864,256]{1,0:T(8,128)} %shard_map.82), kind=kLoop, calls=%fused_computation | loop fusion | flops 221184 | bytes 1769472 | tf_op jit(solution)/shard_map/mul | solution.py:568
